TPU v7x, 128 devices: a whole 4x4x4 slice. The times are simulated.
128 devices in a mesh: scen: 16 (over y_hi, z, core), dec: 8 (over y_lo, x).
Axes of the slice: x: 4, y: 4 (y_hi: 2, y_lo: 2; y = y_hi * 2 + y_lo), z: 4, core: 2. Of those that a mesh axis runs over, the one named last changes fastest.
Arguments:
- order_qty: bfloat16 [8192, 8192], P('dec', 'scen'), may hold values from 0 to 2
- multiplier: float32 [8192, 8192], P('dec', 'scen'), may hold values from -6 to 6
- unit_cost: bfloat16 [8192, 8192], P('dec', 'scen'), may hold values from -6 to 6
- demand: bfloat16 [2048, 8192], P('dec', 'scen'), may hold values from -6 to 6
- technology: bfloat16 [8192, 2048], P('dec'), may hold values from -0.0625 to 0.0625
- kkt_inverse: bfloat16 [2048, 2048], P('dec'), may hold values from -1 to 3
- probability: float32 [8192], P('scen'), may hold values from 0.1 to 1
- scenario_node: int32 [8192, 1], P('scen'), may hold values from 0 to 511
Outputs:
- planned: bfloat16 [8192, 8192], P('dec', 'scen')
- recourse: bfloat16 [2048, 8192], P('dec', 'scen')
- consensus: float32 [8192, 512], P('dec')
- multiplier_next: float32 [8192, 8192], P('dec', 'scen')
Inputs may be any that keep to these rules, and one draw needn't show every extreme that they name: `scenario_node`: every one of the 512 nodes is the node of some scenario.
All inputs are finite; a program needn't handle non-finite values.
Results may differ from a plain program's by a relative error of at most 0.023.
Values may be sent and summed in bfloat16 or wider, within the bound.
A program may use at most 64 MiB of HBM per device.

v0:
```python
import jax
import jax.numpy as jnp
from jax import lax
from jax.sharding import PartitionSpec as P

G = 512


step_size = 0.5
penalty = 2.0


def swapped(value, axis, stride):
    mask = 2**stride
    pairs = [(source, source ^ mask) for source in range(lax.axis_size(axis))]
    return lax.ppermute(value, axis, pairs)


def on_device(
    order_qty, multiplier, unit_cost, demand, technology, kkt_inverse, probability, scenario_node
):
    contract_first = (((0,), (0,)), ((), ()))
    columns = technology
    supply = lax.psum_scatter(
        lax.dot_general(columns, order_qty, contract_first, preferred_element_type=jnp.float32),
        "dec",
        scatter_dimension=0,
        tiled=True,
    )
    right_side = (demand.astype(jnp.float32) - supply).astype(jnp.bfloat16)
    columns = kkt_inverse
    solved = jnp.dot(
        columns,
        lax.all_gather(right_side, "dec", axis=0, tiled=True),
        preferred_element_type=jnp.float32,
    )
    recourse = solved.astype(jnp.bfloat16)
    columns = technology
    linked = jnp.dot(
        columns,
        lax.all_gather(recourse, "dec", axis=0, tiled=True),
        preferred_element_type=jnp.float32,
    )
    gradient = unit_cost.astype(jnp.float32) + multiplier + linked
    planned = jnp.maximum(order_qty.astype(jnp.float32) - step_size * gradient, 0.0).astype(
        jnp.bfloat16
    )
    node_list = scenario_node[:, 0]
    node_ids = jnp.arange(G, dtype=jnp.int32)
    member = (node_list[:, None] == node_ids[None, :]).astype(jnp.float32)
    weight_table = member * probability[:, None]
    weight_high = weight_table.astype(jnp.bfloat16)
    weight_low = (weight_table - weight_high.astype(jnp.float32)).astype(jnp.bfloat16)
    totals = jnp.dot(planned, weight_high, preferred_element_type=jnp.float32)
    totals = totals + jnp.dot(planned, weight_low, preferred_element_type=jnp.float32)
    masses = jnp.dot(probability, member, precision=lax.Precision.HIGHEST)
    rounds = lax.axis_size("scen").bit_length() - 1
    for bit_index in range(rounds):
        other_totals, other_masses = swapped((totals, masses), "scen", bit_index)
        totals = totals + other_totals
        masses = masses + other_masses
    consensus = totals / masses[None, :]
    spread_back = jnp.take(consensus, node_list, axis=1)
    multiplier_next = multiplier + penalty * (planned.astype(jnp.float32) - spread_back)
    return (planned, recourse, consensus, multiplier_next)


def solution(mesh):
    placed = (
        P("dec", "scen"),
        P("dec", "scen"),
        P("dec", "scen"),
        P("dec", "scen"),
        P("dec", None),
        P("dec", None),
        P("scen"),
        P("scen", None),
    )
    return jax.shard_map(
        on_device,
        mesh=mesh,
        in_specs=placed,
        out_specs=(P("dec", "scen"), P("dec", "scen"), P("dec", None), P("dec", "scen")),
        check_vma=False,
    )
```

profile of v0, /device:TPU:1, one launch (start us, length us, event | category | flops | bytes accessed | tf_op | source)
XLA Modules:
  0.0 339.6 jit_solution(1351246959328302948)
XLA Ops:
  7.2 0.0 copy-start
  7.2 0.0 reduce-scatter.2.cloned.1.call-start
  7.2 6.9 %fusion.20 = f32[2048,512]{1,0:T(8,128)} fusion(bf16[1024,2048]{1,0:T(8,128)(2,1)} %param.12, bf16[1024,512]{1,0:T(8,128)(2,1)} %param.8), kind=kOutput, calls=%fused_computation.32 | convolution fusion | flops 2147483648 | bytes 9437184 | tf_op jit(solution)/shard_map/dot_general | solution.py:25
  14.1 0.0 reduce-scatter.2.cloned.1.call-update
  14.1 0.0 all-gather.3.cloned.1.call-start
  14.2 56.4 %reduce-scatter.2.cloned.1.call-done = f32[256,512]{1,0:T(8,128)} async-done(((f32[2048,512]{1,0:T(8,128)}), f32[256,512]{1,0:T(8,128)}) %reduce-scatter.2.cloned.1.call-update) | async-done | bytes 524304 | tf_op jit(solution)/shard_map/reduce_scatter | solution.py:24
  70.6 0.0 copy-done.5
  70.6 1.8 subtract_convert_fusion
  72.4 0.0 all-gather.3.cloned.1.call-update
  72.4 0.0 all-gather.5.cloned.1.call-start
  72.5 35.4 %all-gather.3.cloned.1.call-done = bf16[2048,512]{1,0:T(8,128)(2,1)} async-done(((bf16[256,512]{1,0:T(8,128)(2,1)}), bf16[2048,512]{1,0:T(8,128)(2,1)}) %all-gather.3.cloned.1.call-update) | async-done | bytes 2097168 | tf_op jit(solution)/shard_map/all_gather | solution.py:34
  107.9 3.0 fusion.6
  110.9 0.0 all-gather.5.cloned.1.call-update
  111.0 2.4 copy.12
  113.4 1.8 copy.14
  115.2 2.4 copy.13
  117.5 39.0 %all-gather.5.cloned.1.call-done = bf16[2048,512]{0,1:T(8,128)(2,1)} async-done(((bf16[256,512]{0,1:T(8,128)(2,1)}), bf16[2048,512]{0,1:T(8,128)(2,1)}) %all-gather.5.cloned.1.call-update) | async-done | bytes 2097168 | tf_op jit(solution)/shard_map/all_gather | solution.py:41
  156.5 6.3 %fusion.5 = bf16[1024,512]{0,1:T(8,128)(2,1)S(1)} fusion(f32[1024,512]{0,1:T(8,128)} %copy.14, bf16[1024,512]{0,1:T(8,128)(2,1)} %copy.13, bf16[1024,512]{0,1:T(8,128)(2,1)S(1)} %copy-done.3, bf16[2048,512]{0,1:T(8,128)(2,1)} %all-gather.5.cloned.1.call-done, bf16[1024,2048]{1,0:T(8,128)(2,1)} %param.12), kind=kOutput, calls=%fused_computation.8 | convolution fusion | flops 2151677952 | bytes 11534336 | tf_op jit(solution)/shard_map/dot_general | solution.py:39
  162.8 0.8 fusion.9
  163.6 0.8 convolution_add_fusion
  164.5 5.2 %collective-permute-start = (f32[1024,512]{1,0:T(8,128)S(1)}, f32[1024,512]{1,0:T(8,128)S(1)}, u32[]{:S(2)}, u32[]{:S(2)}) collective-permute-start(f32[1024,512]{1,0:T(8,128)S(1)} %convolution_add_fusion), channel_id=1, source_target_pairs={{0,8},{8,0},{16,24},{24,16},{32,40},{40,32},{48,56},{56,48},{64,72... | collective-permute-start | bytes 6291464 | tf_op jit(solution)/shard_map/ppermute | solution.py:16
  169.7 3.8 %collective-permute-done = f32[1024,512]{1,0:T(8,128)S(1)} collective-permute-done((f32[1024,512]{1,0:T(8,128)S(1)}, f32[1024,512]{1,0:T(8,128)S(1)}, u32[]{:S(2)}, u32[]{:S(2)}) %collective-permute-start) | collective-permute-done | bytes 2097184 | tf_op jit(solution)/shard_map/ppermute | solution.py:16
  173.5 0.5 add.51
  174.0 0.5 collective-permute-start.1
  174.4 46.4 %collective-permute-done.1 = f32[1024,512]{1,0:T(8,128)S(1)} collective-permute-done((f32[1024,512]{1,0:T(8,128)S(1)}, f32[1024,512]{1,0:T(8,128)S(1)}, u32[]{:S(2)}, u32[]{:S(2)}) %collective-permute-start.1) | collective-permute-done | bytes 2097184 | tf_op jit(solution)/shard_map/ppermute | solution.py:16
  220.9 0.5 add.52
  221.4 0.0 copy-start.4
  221.4 2.1 collective-permute-start.2
  223.5 45.4 %collective-permute-done.2 = f32[1024,512]{1,0:T(8,128)S(1)} collective-permute-done((f32[1024,512]{1,0:T(8,128)S(1)}, f32[1024,512]{1,0:T(8,128)S(1)}, u32[]{:S(2)}, u32[]{:S(2)}) %collective-permute-start.2) | collective-permute-done | bytes 2097184 | tf_op jit(solution)/shard_map/ppermute | solution.py:16
  268.9 1.8 add.53
  270.7 2.1 collective-permute-start.3
  272.8 0.5 fusion.8
  273.3 2.4 collective-permute-start.4
  275.7 0.8 collective-permute-done.4
  276.5 1.3 collective-permute-start.5
  277.8 1.6 collective-permute-done.5
  279.4 2.9 collective-permute-start.6
  282.3 1.4 collective-permute-done.6
  283.7 0.4 collective-permute-start.7
  284.2 33.4 %collective-permute-done.7 = f32[512]{0:T(512)S(1)} collective-permute-done((f32[512]{0:T(512)S(1)}, f32[512]{0:T(512)S(1)}, u32[]{:S(2)}, u32[]{:S(2)}) %collective-permute-start.7) | collective-permute-done | bytes 2080 | tf_op jit(solution)/shard_map/ppermute | solution.py:16
  317.5 0.8 copy.18
  318.4 1.3 copy.17
  319.7 0.0 collective-permute-done.3
  319.7 4.0 %add_divide_fusion = f32[1024,512]{1,0:T(8,128)} fusion(f32[1024,512]{1,0:T(8,128)} %add.53, f32[1024,512]{1,0:T(8,128)} %collective-permute-done.3, f32[512]{0:T(512)S(1)} %add.58), kind=kLoop, calls=%fused_computation.9 | loop fusion | flops 1048576 | bytes 6293504 | tf_op jit(solution)/shard_map/div | solution.py:62
  323.8 1.9 copy.15
  325.7 2.7 gather_fusion
  328.4 2.9 fusion.1
  331.3 1.8 copy.19
  (19 shorter events, 0.1 us)
Async XLA Ops:
  7.2 100.7 %copy-start = (bf16[256,2048]{1,0:T(8,128)(2,1)S(1)}, bf16[256,2048]{1,0:T(8,128)(2,1)}, u32[]{:S(2)}) copy-start(bf16[256,2048]{1,0:T(8,128)(2,1)} %param.13) | copy-start | bytes 3145732
  7.2 63.4 %reduce-scatter.2.cloned.1.call-start = ((), (), s32[]{:S(2)}) async-start(), calls=%async_computation.1 | async-start | bytes 4718592 | tf_op jit(solution)/shard_map/reduce_scatter | solution.py:24
  14.1 56.5 %copy-start.5 = (bf16[256,512]{1,0:T(8,128)(2,1)S(1)}, bf16[256,512]{1,0:T(8,128)(2,1)}, u32[]{:S(2)}) copy-start(bf16[256,512]{1,0:T(8,128)(2,1)} %param.11) | copy-start | bytes 786436
  14.1 93.7 %all-gather.3.cloned.1.call-start = ((), (), s32[]{:S(2)}) async-start(), calls=%async_computation.2 | async-start | bytes 2359296 | tf_op jit(solution)/shard_map/all_gather | solution.py:34
  72.4 84.0 %all-gather.5.cloned.1.call-start = ((), (), s32[]{:S(2)}) async-start(), calls=%async_computation.3 | async-start | bytes 2359296 | tf_op jit(solution)/shard_map/all_gather | solution.py:41
  110.9 2.4 copy-start.2
  115.2 41.3 %copy-start.3 = (bf16[1024,512]{0,1:T(8,128)(2,1)S(1)}, bf16[1024,512]{0,1:T(8,128)(2,1)}, u32[]{:S(2)}) copy-start(bf16[1024,512]{0,1:T(8,128)(2,1)} %copy.12) | copy-start | bytes 3145732
  117.5 45.2 %copy-start.6 = (s32[512,1]{0,1:T(1,128)S(1)}, s32[512,1]{0,1:T(1,128)}, u32[]{:S(2)}) copy-start(s32[512,1]{0,1:T(1,128)} %param.15) | copy-start | bytes 6148
  117.5 45.3 %copy-start.7 = (f32[512]{0:T(512)S(1)}, f32[512]{0:T(512)}, u32[]{:S(2)}) copy-start(f32[512]{0:T(512)} %param.14) | copy-start | bytes 6148
  162.8 155.6 %copy-start.1 = (bf16[1024,512]{0,1:T(8,128)(2,1)}, bf16[1024,512]{0,1:T(8,128)(2,1)S(1)}, u32[]{:S(2)}) copy-start(bf16[1024,512]{0,1:T(8,128)(2,1)S(1)} %fusion.5) | copy-start | bytes 3145732
  164.5 9.0 %collective-permute-start = (f32[1024,512]{1,0:T(8,128)S(1)}, f32[1024,512]{1,0:T(8,128)S(1)}, u32[]{:S(2)}, u32[]{:S(2)}) collective-permute-start(f32[1024,512]{1,0:T(8,128)S(1)} %convolution_add_fusion), channel_id=1, source_target_pairs={{0,8},{8,0},{16,24},{24,16},{32,40},{40,32},{48,56},{56,48},{64,72... | collective-permute-start | bytes 6291464 | tf_op jit(solution)/shard_map/ppermute | solution.py:16
  174.0 46.9 %collective-permute-start.1 = (f32[1024,512]{1,0:T(8,128)S(1)}, f32[1024,512]{1,0:T(8,128)S(1)}, u32[]{:S(2)}, u32[]{:S(2)}) collective-permute-start(f32[1024,512]{1,0:T(8,128)S(1)} %add.51), channel_id=1, source_target_pairs={{0,16},{8,24},{16,0},{24,8},{32,48},{40,56},{48,32},{56,40},{64,80... | collective-permute-start | bytes 6291464 | tf_op jit(solution)/shard_map/ppermute | solution.py:16
  221.4 96.2 %copy-start.4 = (bf16[256,512]{0,1:T(8,128)(2,1)S(1)}, bf16[256,512]{0,1:T(8,128)(2,1)}, u32[]{:S(2)}) copy-start(bf16[256,512]{0,1:T(8,128)(2,1)} %fusion.6) | copy-start | bytes 786436
  221.4 47.5 %collective-permute-start.2 = (f32[1024,512]{1,0:T(8,128)S(1)}, f32[1024,512]{1,0:T(8,128)S(1)}, u32[]{:S(2)}, u32[]{:S(2)}) collective-permute-start(f32[1024,512]{1,0:T(8,128)S(1)} %add.52), channel_id=1, source_target_pairs={{0,32},{8,40},{16,48},{24,56},{32,0},{40,8},{48,16},{56,24},{64,96... | collective-permute-start | bytes 6291464 | tf_op jit(solution)/shard_map/ppermute | solution.py:16
  270.7 49.0 %collective-permute-start.3 = (f32[1024,512]{1,0:T(8,128)}, f32[1024,512]{1,0:T(8,128)}, u32[]{:S(2)}, u32[]{:S(2)}) collective-permute-start(f32[1024,512]{1,0:T(8,128)} %add.53), channel_id=1, source_target_pairs={{0,64},{8,72},{16,80},{24,88},{32,96},{40,104},{48,112},{56,120},{... | collective-permute-start | bytes 6291464 | tf_op jit(solution)/shard_map/ppermute | solution.py:16
  273.3 3.2 collective-permute-start.4
  276.5 2.8 collective-permute-start.5
  279.4 4.3 %collective-permute-start.6 = (f32[512]{0:T(512)S(1)}, f32[512]{0:T(512)S(1)}, u32[]{:S(2)}, u32[]{:S(2)}) collective-permute-start(f32[512]{0:T(512)S(1)} %add.56), channel_id=1, source_target_pairs={{0,32},{8,40},{16,48},{24,56},{32,0},{40,8},{48,16},{56,24},{64,96... | collective-permute-start | bytes 6152 | tf_op jit(solution)/shard_map/ppermute | solution.py:16
  283.7 33.8 %collective-permute-start.7 = (f32[512]{0:T(512)S(1)}, f32[512]{0:T(512)S(1)}, u32[]{:S(2)}, u32[]{:S(2)}) collective-permute-start(f32[512]{0:T(512)S(1)} %add.57), channel_id=1, source_target_pairs={{0,64},{8,72},{16,80},{24,88},{32,96},{40,104},{48,112},{56,120},{... | collective-permute-start | bytes 6152 | tf_op jit(solution)/shard_map/ppermute | solution.py:16
Sparse Core Ops, SparseCore 0:
  14.3 56.2 reduce-scatter.1
  72.8 35.0 all-gather.2
  111.1 45.3 all-gather.4
where the time goes:
time: 341 us; the launch traced here: 340 us
  waiting for transfers between devices  264 us (77%)
  matrix products  18.3 us (5%)
  starting transfers between devices  17 us (5%)
  local copies, waits for them, and re-layouts  15.2 us (4%)
  between operations  13.8 us (4%)
  other arithmetic  11.6 us (3%)
    ppermute x8, waiting for transfers between devices, swapped(): return lax.ppermute(value, axis, pairs)  133 us
    reduce_scatter x1, waiting for transfers between devices, on_device(): lax.psum_scatter(lax.dot_general(columns, order_qty, contract_first, pref...  56.4 us
    all_gather x1, waiting for transfers between devices, on_device(): lax.all_gather(recourse, 'dec', axis=0, tiled=True)  39 us
    all_gather x1, waiting for transfers between devices, on_device(): lax.all_gather(right_side, 'dec', axis=0, tiled=True)  35.4 us
    ppermute x8, starting transfers between devices, swapped(): return lax.ppermute(value, axis, pairs)  16.9 us
    unnamed x22, local copies, waits for them, and re-layouts  10.6 us
    dot_general x1, matrix products, on_device(): lax.dot_general(columns, order_qty, contract_first, preferred_element_typ...  6.89 us
  transfers between devices with their start and end apart: 11, of which 10 were waited for; matrix products, arithmetic and copies ran while one was open for 3% of the time, Pallas kernels for 0%

commit v1 on v0

v1 whole, which is shorter than its diff:
```python
import jax
import jax.numpy as jnp
from jax import lax
from jax.experimental import pallas as pl
from jax.experimental.pallas import tpu as pltpu
from jax.sharding import PartitionSpec as P

G = 512
STEP = 0.5
PENALTY = 2.0

ROWS = 1024
S = 512
M = 2048
B = 256
HALF = 512
SLICE = 64

RA = 288
HA = RA // 2
RB = S - RA
HB = RB // 2

bf16 = jnp.bfloat16
f32 = jnp.float32
MESH = pl.DeviceIdType.MESH


def nt(a, b):
    return lax.dot_general(a, b, (((1,), (1,)), ((), ())), preferred_element_type=f32)


def nn(a, b):
    return jnp.dot(a, b, preferred_element_type=f32)


def kernel(
    order_hbm, mult_hbm, cost_hbm, demand_hbm, tech_hbm, kkt_hbm, prob_ref, node_ref,
    planned_out, recourse_out, cons_out, next_out,
    order_v, order_t, mult_v, cost_v, demand_v, tech_v, kkt_v,
    part,
    a1_s, a1_r, a2_s, a2_r, a3_s, a3_r,
    b1_s, b1_r, b2_s, b2_r, b3_s, b3_r,
    rhs, rec, rec_own,
    weight, member, mass_s, mass_r, mass_c, mass_p,
    planned_v, tot, e1_s, e1_r, e2_s, e2_r, cons_b, cons_f,
    load, tload, out_sem,
    rs_send, rs_recv, ag1_send, ag1_recv, ag2_send, ag2_recv,
    m_send, m_recv, e1_send, e1_recv, e2_send, e2_recv, f_send, f_recv, c_send, c_recv,
):
    s = lax.axis_index("scen")
    d = lax.axis_index("dec")
    x, y = d % 4, d // 4
    core, z, yh = s % 2, (s // 2) % 4, s // 8

    def dec_id(dx, dy):
        return ((y + dy) % 2) * 4 + (x + dx) % 4

    def peer_id(oy, oz):
        return ((yh + oy) % 2) * 4 + (z + oz) % 4

    right, left, across = (s, dec_id(1, 0)), (s, dec_id(3, 0)), (s, dec_id(0, 1))
    twin = (s - core + (1 - core), d)
    offsets = [(1, 0), (0, 2), (1, 2), (0, 1), (0, 3), (1, 1), (1, 3)]

    def peer(oy, oz):
        p = peer_id(oy, oz)
        return (p * 2 + core, d)

    barrier = pltpu.get_barrier_semaphore()
    everyone = [right, left, across, twin] + [peer(oy, oz) for oy, oz in offsets]
    for other in everyone:
        pl.semaphore_signal(barrier, inc=1, device_id=other, device_id_type=MESH)

    started = []

    def send(src, dst, ssem, rsem, k, target):
        copy = pltpu.make_async_remote_copy(
            src_ref=src, dst_ref=dst, send_sem=ssem.at[k], recv_sem=rsem.at[k],
            device_id=target, device_id_type=MESH,
        )
        copy.start()
        started.append(copy)
        return copy

    load_order = pltpu.make_async_copy(order_hbm, order_v, load.at[0])
    load_order.start()

    def tech_copy(r):
        dy, dx = tech_at(r)
        cols = pl.ds(pl.multiple_of(dec_id(dx, dy) * B, B), B)
        return pltpu.make_async_copy(tech_hbm.at[:, cols], tech_v.at[:, cols], tload.at[r])

    def tech_at(r):
        if r < 2:
            return 1 - r, 2
        return (1 if r < 5 else 0), (1 - (r - 2) % 3) % 4

    for r in range(8):
        tech_copy(r).start()
    others = [
        pltpu.make_async_copy(demand_hbm, demand_v, load.at[1]),
        pltpu.make_async_copy(kkt_hbm, kkt_v, load.at[2]),
        pltpu.make_async_copy(mult_hbm, mult_v, load.at[3]),
        pltpu.make_async_copy(cost_hbm, cost_v, load.at[4]),
    ]
    for copy in others:
        copy.start()

    load_order.wait()
    order_t[...] = order_v[...].T

    def first_product(dy, dx):
        cols = pl.ds(pl.multiple_of(dec_id(dx, dy) * B, B), B)
        part[dy, dx] = nn(order_t[...], tech_v[:, cols])

    tech_copy(0).wait()
    tech_copy(1).wait()

    @pl.loop(0, 2)
    def _(i):
        first_product(1 - i, 2)

    for dy in range(2):
        a1_s[0, dy] = part[dy, 2, 0:HA].astype(bf16)
        a1_s[1, dy] = part[dy, 2, HA:RA].astype(bf16)
    b1_s[2] = part[1, 2, RA:S].astype(bf16)

    pl.semaphore_wait(barrier, len(everyone))

    a1 = [
        send(a1_s.at[0], a1_r.at[0], rs_send, rs_recv, 0, right),
        send(a1_s.at[1], a1_r.at[1], rs_send, rs_recv, 1, left),
    ]
    b1 = {2: send(b1_s.at[2], b1_r.at[2], rs_send, rs_recv, 2, across)}

    for r in range(2, 5):
        tech_copy(r).wait()

    @pl.loop(0, 3)
    def _(i):
        first_product(1, (5 - i) % 4)

    for k, dx in enumerate((1, 3, 0)):
        b1_s[dx] = part[1, dx, RA:S].astype(bf16)
        b1[dx] = send(b1_s.at[dx], b1_r.at[dx], rs_send, rs_recv, 3 + k, across)

    for r in range(5, 8):
        tech_copy(r).wait()

    @pl.loop(0, 3)
    def _(i):
        first_product(0, (5 - i) % 4)

    a1[0].wait_recv()
    a1[1].wait_recv()
    a2 = {}
    for dy in (1, 0):
        a2_s[0, dy, 0:HA] = (part[dy, 1, 0:HA] + a1_r[0, dy].astype(f32)).astype(bf16)
        a2_s[0, dy, HA:RA] = part[dy, 1, HA:RA].astype(bf16)
        a2[0, dy] = send(a2_s.at[0, dy], a2_r.at[0, dy], rs_send, rs_recv, 6 + dy, right)
        a2_s[1, dy, 0:HA] = part[dy, 3, 0:HA].astype(bf16)
        a2_s[1, dy, HA:RA] = (part[dy, 3, HA:RA] + a1_r[1, dy].astype(f32)).astype(bf16)
        a2[1, dy] = send(a2_s.at[1, dy], a2_r.at[1, dy], rs_send, rs_recv, 8 + dy, left)
        if dy == 1:
            b1[2].wait_recv()
            b2_s[0] = (part[0, 2, RA:RA + HB] + b1_r[2, 0:HB].astype(f32)).astype(bf16)
            b2_s[1] = (part[0, 2, RA + HB:S] + b1_r[2, HB:RB].astype(f32)).astype(bf16)
            b2 = [
                send(b2_s.at[0], b2_r.at[0], rs_send, rs_recv, 10, right),
                send(b2_s.at[1], b2_r.at[1], rs_send, rs_recv, 11, left),
            ]

    node_ids = lax.broadcasted_iota(jnp.int32, (G, S), 0)
    same = node_ids == node_ref[...]
    member[...] = jnp.where(same, 1.0, 0.0).astype(bf16)
    weight[...] = jnp.where(same, prob_ref[...], 0.0).astype(bf16)
    mass_s[...] = nt(jnp.ones((16, S), bf16), weight[...])[0:8]
    mass_twin = send(mass_s, mass_r, m_send, m_recv, 0, twin)
    for copy in others:
        copy.wait()

    b1[1].wait_recv()
    b2[0].wait_recv()
    b3_s[0, 0:HB] = (
        part[0, 1, RA:RA + HB] + b1_r[1, 0:HB].astype(f32) + b2_r[0].astype(f32)
    ).astype(bf16)
    b3_s[0, HB:RB] = (part[0, 1, RA + HB:S] + b1_r[1, HB:RB].astype(f32)).astype(bf16)
    b3 = [send(b3_s.at[0], b3_r.at[0], rs_send, rs_recv, 12, right)]
    b1[3].wait_recv()
    b2[1].wait_recv()
    b3_s[1, 0:HB] = (part[0, 3, RA:RA + HB] + b1_r[3, 0:HB].astype(f32)).astype(bf16)
    b3_s[1, HB:RB] = (
        part[0, 3, RA + HB:S] + b1_r[3, HB:RB].astype(f32) + b2_r[1].astype(f32)
    ).astype(bf16)
    b3.append(send(b3_s.at[1], b3_r.at[1], rs_send, rs_recv, 13, left))

    a2[0, 1].wait_recv()
    a2[1, 1].wait_recv()
    a3_s[...] = (
        part[1, 0, 0:RA] + a2_r[0, 1].astype(f32) + a2_r[1, 1].astype(f32)
    ).astype(bf16)
    a3 = send(a3_s, a3_r, rs_send, rs_recv, 14, across)

    mass_twin.wait_recv()
    mass_c[...] = mass_s[...] + mass_r[...]
    mass_copies = [
        send(mass_c, mass_p.at[k], m_send, m_recv, 1 + k, peer(oy, oz))
        for k, (oy, oz) in enumerate(offsets)
    ]

    demand_t = demand_v[...].T
    own = pl.ds(pl.multiple_of(d * B, B), B)
    b1[0].wait_recv()
    b3[0].wait_recv()
    b3[1].wait_recv()
    rhs[RA:S, own] = (
        demand_t[RA:S].astype(f32)
        - (
            part[0, 0, RA:S] + b1_r[0].astype(f32)
            + b3_r[0].astype(f32) + b3_r[1].astype(f32)
        )
    ).astype(bf16)

    low0, low1 = (0, HA), (HA, HA)
    low = (0, RA)
    high = (RA, RB)
    high0, high1 = (RA, HB), (RA + HB, HB)

    def gatherer(buf, ssem, rsem):
        def go(rows, dx, dy, target, k):
            cols = pl.ds(pl.multiple_of(dec_id(dx, dy) * B, B), B)
            where = buf.at[pl.ds(*rows), cols]
            return send(where, where, ssem, rsem, k, target)

        c = {}

        def start_high():
            c[0] = go(high, 0, 0, right, 0)
            c[1] = go(high, 0, 0, left, 1)
            c[2] = go(high, 0, 0, across, 2)

        def start_low():
            c[9] = go(low, 0, 0, across, 9)
            c[10] = go(low, 0, 0, right, 10)
            c[11] = go(low, 0, 0, left, 11)

        def first_turn():
            c[0].wait_recv()
            c[3] = go(high0, 3, 0, right, 3)
            c[5] = go(high, 3, 0, across, 5)
            c[1].wait_recv()
            c[4] = go(high1, 1, 0, left, 4)
            c[6] = go(high, 1, 0, across, 6)

        def rest():
            c[9].wait_recv()
            c[12] = go(low, 0, 1, right, 12)
            c[13] = go(low, 0, 1, left, 13)
            c[3].wait_recv()
            c[7] = go(high0, 2, 0, across, 7)
            c[4].wait_recv()
            c[8] = go(high1, 2, 0, across, 8)
            c[10].wait_recv()
            c[14] = go(low0, 3, 0, right, 14)
            c[11].wait_recv()
            c[15] = go(low1, 1, 0, left, 15)
            c[12].wait_recv()
            c[16] = go(low0, 3, 1, right, 16)
            c[13].wait_recv()
            c[17] = go(low1, 1, 1, left, 17)

        def end_high():
            for k in (2, 5, 6, 7, 8):
                c[k].wait_recv()

        def end_low():
            for k in (14, 15, 16, 17):
                c[k].wait_recv()

        return start_high, start_low, first_turn, rest, end_high, end_low

    high_1, low_1, turn_1, rest_1, end_high_1, end_low_1 = gatherer(rhs, ag1_send, ag1_recv)
    high_2, low_2, turn_2, rest_2, end_high_2, end_low_2 = gatherer(rec, ag2_send, ag2_recv)

    high_1()
    a2[0, 0].wait_recv()
    a2[1, 0].wait_recv()
    a3.wait_recv()
    rhs[0:RA, own] = (
        demand_t[0:RA].astype(f32)
        - (
            part[0, 0, 0:RA] + a2_r[0, 0].astype(f32)
            + a2_r[1, 0].astype(f32) + a3_r[...].astype(f32)
        )
    ).astype(bf16)
    low_1()
    turn_1()
    rest_1()
    end_high_1()
    rec[RA:S, own] = nt(rhs[RA:S], kkt_v[...]).astype(bf16)
    high_2()
    end_low_1()
    rec[0:RA, own] = nt(rhs[0:RA], kkt_v[...]).astype(bf16)
    low_2()
    rec_own[...] = nt(kkt_v[...], rhs[...]).astype(bf16)
    write_rec = pltpu.make_async_copy(rec_own, recourse_out, out_sem.at[0])
    write_rec.start()
    turn_2()
    rest_2()
    end_high_2()
    end_low_2()

    CH = 128

    def plan(rows):
        linked = nt(tech_v[rows, :], rec[...])
        gradient = cost_v[rows, :].astype(f32) + mult_v[rows, :] + linked
        planned = jnp.maximum(order_v[rows, :].astype(f32) - STEP * gradient, 0.0).astype(bf16)
        planned_v[rows, :] = planned
        return nt(planned, weight[...])

    def core_copy(j):
        rows = pl.ds(pl.multiple_of(j * CH, CH), CH)
        return pltpu.make_async_remote_copy(
            src_ref=e1_s.at[rows], dst_ref=e1_r.at[rows],
            send_sem=e1_send.at[j], recv_sem=e1_recv.at[j],
            device_id=twin, device_id_type=MESH,
        )

    @pl.loop(0, HALF // CH)
    def _(j):
        rows = pl.ds(pl.multiple_of((1 - core) * HALF + j * CH, CH), CH)
        e1_s[pl.ds(pl.multiple_of(j * CH, CH), CH), :] = plan(rows).astype(bf16)
        core_copy(j).start()

    @pl.loop(0, HALF // CH)
    def _(j):
        rows = pl.ds(pl.multiple_of(core * HALF + j * CH, CH), CH)
        here = pl.ds(pl.multiple_of(j * CH, CH), CH)
        mine = plan(rows)
        core_copy(j).wait_recv()
        total = mine + e1_r[here, :].astype(f32)
        tot[here, :] = total
        e2_s[here, :] = total.astype(bf16)

    def slice_of(p):
        return pl.ds(pl.multiple_of(p * SLICE, SLICE), SLICE)

    e2 = [
        send(e2_s.at[slice_of(peer_id(oy, oz))], e2_r.at[k], e2_send, e2_recv, k, peer(oy, oz))
        for k, (oy, oz) in enumerate(offsets)
    ]
    write_planned = pltpu.make_async_copy(planned_v, planned_out, out_sem.at[1])
    write_planned.start()
    me = peer_id(0, 0)
    mass = mass_c[...]
    for k in range(7):
        mass_copies[k].wait_recv()
        mass = mass + mass_p[k]
    total = tot[slice_of(me), :]
    for k in range(7):
        e2[k].wait_recv()
        total = total + e2_r[k].astype(f32)

    def cons_at(c, p):
        return pl.ds(pl.multiple_of(c * HALF + p * SLICE, SLICE), SLICE)

    mine = cons_at(core, me)
    cons_b[mine, :] = (total / mass[0:1, :]).astype(bf16)
    f = [
        send(cons_b.at[mine], cons_b.at[mine], f_send, f_recv, k, peer(oy, oz))
        for k, (oy, oz) in enumerate(offsets)
    ]
    c = [send(cons_b.at[mine], cons_b.at[mine], c_send, c_recv, 7, twin)]
    for k, (oy, oz) in enumerate(offsets):
        f[k].wait_recv()
        theirs = cons_at(core, peer_id(oy, 4 - oz))
        c.append(send(cons_b.at[theirs], cons_b.at[theirs], c_send, c_recv, k, twin))

    def finish(which):
        @pl.loop(0, HALF // CH)
        def _(j):
            rows = pl.ds(pl.multiple_of(which * HALF + j * CH, CH), CH)
            spread = nn(cons_b[rows, :], member[...])
            cons_f[rows, :] = cons_b[rows, :].astype(f32)
            mult_v[rows, :] = mult_v[rows, :] + PENALTY * (planned_v[rows, :].astype(f32) - spread)

        both = pl.ds(pl.multiple_of(which * HALF, HALF), HALF)
        return both

    writes = []

    def put(both, k):
        writes.append(pltpu.make_async_copy(cons_f.at[both], cons_out.at[both], out_sem.at[2 + k]))
        writes.append(pltpu.make_async_copy(mult_v.at[both], next_out.at[both], out_sem.at[4 + k]))
        writes[-1].start()
        writes[-2].start()

    put(finish(core), 0)
    for copy in c:
        copy.wait_recv()
    put(finish(1 - core), 1)

    for copy in started:
        copy.wait_send()
    for j in range(HALF // CH):
        core_copy(j).wait_send()
    write_rec.wait()
    write_planned.wait()
    for copy in writes:
        copy.wait()


def on_device(
    order_qty, multiplier, unit_cost, demand, technology, kkt_inverse, probability, scenario_node
):
    any_space = pl.BlockSpec(memory_space=pl.ANY)
    vmem = pl.BlockSpec(memory_space=pltpu.VMEM)
    V = pltpu.VMEM
    D = pltpu.SemaphoreType.DMA
    scratch = [
        V((ROWS, S), bf16), V((S, ROWS), bf16), V((ROWS, S), f32), V((ROWS, S), bf16),
        V((B, S), bf16), V((ROWS, M), bf16), V((B, M), bf16),
        V((2, 4, S, B), f32),
        V((2, 2, HA, B), bf16), V((2, 2, HA, B), bf16),
        V((2, 2, RA, B), bf16), V((2, 2, RA, B), bf16),
        V((RA, B), bf16), V((RA, B), bf16),
        V((4, RB, B), bf16), V((4, RB, B), bf16),
        V((2, HB, B), bf16), V((2, HB, B), bf16),
        V((2, RB, B), bf16), V((2, RB, B), bf16),
        V((S, M), bf16), V((S, M), bf16), V((B, S), bf16),
        V((G, S), bf16), V((G, S), bf16),
        V((8, G), f32), V((8, G), f32), V((8, G), f32), V((7, 8, G), f32),
        V((ROWS, S), bf16), V((HALF, G), f32), V((HALF, G), bf16), V((HALF, G), bf16),
        V((HALF, G), bf16), V((7, SLICE, G), bf16), V((ROWS, G), bf16), V((ROWS, G), f32),
        D((5,)), D((8,)), D((6,)),
        D((15,)), D((15,)), D((18,)), D((18,)), D((18,)), D((18,)),
        D((8,)), D((8,)), D((4,)), D((4,)), D((7,)), D((7,)), D((7,)), D((7,)), D((8,)), D((8,)),
    ]
    return tuple(
        pl.pallas_call(
            kernel,
            out_shape=(
                jax.ShapeDtypeStruct((ROWS, S), bf16),
                jax.ShapeDtypeStruct((B, S), bf16),
                jax.ShapeDtypeStruct((ROWS, G), f32),
                jax.ShapeDtypeStruct((ROWS, S), f32),
            ),
            in_specs=[any_space] * 6 + [vmem] * 2,
            out_specs=(any_space,) * 4,
            scratch_shapes=scratch,
            compiler_params=pltpu.CompilerParams(
                collective_id=0, has_side_effects=True, vmem_limit_bytes=56 * 2**20
            ),
        )(
            order_qty, multiplier, unit_cost, demand, technology, kkt_inverse,
            probability.reshape(1, S), scenario_node.reshape(1, S),
        )
    )


def solution(mesh):
    placed = (
        P("dec", "scen"),
        P("dec", "scen"),
        P("dec", "scen"),
        P("dec", "scen"),
        P("dec", None),
        P("dec", None),
        P("scen"),
        P("scen", None),
    )
    return jax.shard_map(
        on_device,
        mesh=mesh,
        in_specs=placed,
        out_specs=(P("dec", "scen"), P("dec", "scen"), P("dec", None), P("dec", "scen")),
        check_vma=False,
    )
```

time: 341 us -> 94.7 us (0.28)
  waiting for transfers between devices: 264 us -> 0 us
  Pallas kernels: 0 us -> 86.1 us
  matrix products: 18.3 us -> 0 us
  starting transfers between devices: 17 us -> 0 us
  between operations: 13.8 us -> 0.65 us
  other arithmetic: 11.6 us -> 0 us
  local copies, waits for them, and re-layouts: 15.2 us -> 7.75 us
    ppermute x8 -> x0, waiting for transfers between devices: 133 us -> none  [swapped(): return lax.ppermute(value, axis, pairs)]
    pallas_call x0 -> x1, Pallas kernels: none -> 86.1 us  [on_device(): pl.pallas_call(kernel, out_shape=(jax.ShapeDtypeStruct((ROWS, S), bf16),...]
    all_gather x2 -> x0, waiting for transfers between devices: 74.3 us -> none  [the longest x1 39 us: on_device(): lax.all_gather(recourse, 'dec', axis=0, tiled=True)]
    reduce_scatter x1 -> x0, waiting for transfers between devices: 56.4 us -> none  [on_device(): lax.psum_scatter(lax.dot_general(columns, order_qty, contract_first, pref...]
    dot_general x6 -> x0, matrix products: 18.3 us -> none  [the longest x1 6.89 us: on_device(): lax.dot_general(columns, order_qty, contract_first, preferred_element_typ...]
    ppermute x8 -> x0, starting transfers between devices: 16.9 us -> none  [swapped(): return lax.ppermute(value, axis, pairs)]
    add x8 -> x0, other arithmetic: 5.66 us -> none  [the longest x1 2.9 us: on_device(): multiplier + penalty * (planned.astype(jnp.float32) - spread_back)]
    div x1 -> x0, other arithmetic: 4.05 us -> none  [on_device(): consensus = totals / masses[None, :]]
  transfers between devices with their start and end apart: 11 -> 0, of which waited for: 10 -> 0; matrix products, arithmetic and copies ran while one was open for 3% -> 0% of each run, Pallas kernels for 0% -> 0%
where the time goes in v1:
time: 94.7 us; the launch traced here: 94.5 us
  Pallas kernels  86.1 us (91%)
  local copies, waits for them, and re-layouts  7.75 us (8%)
    pallas_call x1, Pallas kernels, on_device(): pl.pallas_call(kernel, out_shape=(jax.ShapeDtypeStruct((ROWS, S), bf16),...  86.1 us
    unnamed x8, local copies, waits for them, and re-layouts  7.75 us

profile of v1, /device:TPU:1, one launch (start us, length us, event | category | flops | bytes accessed | tf_op | source)
XLA Modules:
  0.0 94.5 jit_solution(8511329573613432402)
XLA Ops:
  0.6 86.1 %shard_map.111 = (bf16[1024,512]{1,0:T(8,128)(2,1)}, bf16[256,512]{1,0:T(8,128)(2,1)}, f32[1024,512]{1,0:T(8,128)}, f32[1024,512]{1,0:T(8,128)}) custom-call(bf16[1024,512]{1,0:T(8,128)(2,1)} %order_hbm.1, f32[1024,512]{1,0:T(8,128)} %mult_hbm.1, bf16[1024,512]{1,0:T(8,128)(2,1)} %cost_hbm.1, bf16[256,512]{1,0:T(8,128)(2,1)} %demand_hbm.1, ...), custom_call_target="tpu_custom_call" | custom-call | tf_op jit(solution)/shard_map/pallas_call | solution.py:442
  86.8 0.0 copy-start.1
  86.8 2.4 %copy.16 = bf16[1024,512]{1,0:T(8,128)(2,1)} copy(bf16[1024,512]{1,0:T(8,128)(2,1)} %get-tuple-element.8) | data formatting | bytes 2097152
  89.2 1.7 %copy.17 = bf16[256,512]{1,0:T(8,128)(2,1)} copy(bf16[256,512]{1,0:T(8,128)(2,1)} %get-tuple-element.9) | data formatting | bytes 524288
  90.8 0.0 copy-done.1
  90.8 0.0 copy-start
  90.9 1.3 %copy.18 = f32[1024,512]{1,0:T(8,128)} copy(f32[1024,512]{1,0:T(8,128)S(1)} %copy-done.1) | data formatting | bytes 4194304
  92.2 1.0 %copy-done = f32[1024,512]{1,0:T(8,128)S(1)} copy-done((f32[1024,512]{1,0:T(8,128)S(1)}, f32[1024,512]{1,0:T(8,128)}, u32[]{:S(2)}) %copy-start) | copy-done | bytes 2097176
  93.2 1.3 %copy.19 = f32[1024,512]{1,0:T(8,128)} copy(f32[1024,512]{1,0:T(8,128)S(1)} %copy-done) | data formatting | bytes 4194304
Async XLA Ops:
  86.8 4.1 %copy-start.1 = (f32[1024,512]{1,0:T(8,128)S(1)}, f32[1024,512]{1,0:T(8,128)}, u32[]{:S(2)}) copy-start(f32[1024,512]{1,0:T(8,128)} %get-tuple-element.10) | copy-start | bytes 6291460
  90.8 2.3 %copy-start = (f32[1024,512]{1,0:T(8,128)S(1)}, f32[1024,512]{1,0:T(8,128)}, u32[]{:S(2)}) copy-start(f32[1024,512]{1,0:T(8,128)} %get-tuple-element.11) | copy-start | bytes 6291460

commit v2 on v1

--- a/solution.py
+++ b/solution.py
@@ -13,8 +13,8 @@
 S = 512
 M = 2048
 B = 256
-HALF = 512
 SLICE = 64
+CH = 256
 
 RA = 288
 HA = RA // 2
@@ -36,14 +36,14 @@
 
 def kernel(
     order_hbm, mult_hbm, cost_hbm, demand_hbm, tech_hbm, kkt_hbm, prob_ref, node_ref,
-    planned_out, recourse_out, cons_out, next_out,
+    planned_out, recourse_out, cons_out,
     order_v, order_t, mult_v, cost_v, demand_v, tech_v, kkt_v,
     part,
     a1_s, a1_r, a2_s, a2_r, a3_s, a3_r,
     b1_s, b1_r, b2_s, b2_r, b3_s, b3_r,
     rhs, rec, rec_own,
-    weight, member, mass_s, mass_r, mass_c, mass_p,
-    planned_v, tot, e1_s, e1_r, e2_s, e2_r, cons_b, cons_f,
+    weight, mass_s, mass_r,
+    planned_v, tot, e1_s, e1_r, e2_s, e2_r, cons_b,
     load, tload, out_sem,
     rs_send, rs_recv, ag1_send, ag1_recv, ag2_send, ag2_recv,
     m_send, m_recv, e1_send, e1_recv, e2_send, e2_recv, f_send, f_recv, c_send, c_recv,
@@ -61,14 +61,16 @@
 
     right, left, across = (s, dec_id(1, 0)), (s, dec_id(3, 0)), (s, dec_id(0, 1))
     twin = (s - core + (1 - core), d)
-    offsets = [(1, 0), (0, 2), (1, 2), (0, 1), (0, 3), (1, 1), (1, 3)]
+    offsets = [(1, 2), (0, 2), (1, 1), (1, 3), (1, 0), (0, 1), (0, 3)]
 
     def peer(oy, oz):
         p = peer_id(oy, oz)
         return (p * 2 + core, d)
 
+    up, down, over = peer(0, 1), peer(0, 3), peer(1, 0)
+
     barrier = pltpu.get_barrier_semaphore()
-    everyone = [right, left, across, twin] + [peer(oy, oz) for oy, oz in offsets]
+    everyone = [right, left, across, twin, up, down, over]
     for other in everyone:
         pl.semaphore_signal(barrier, inc=1, device_id=other, device_id_type=MESH)
 
@@ -151,6 +153,11 @@
     @pl.loop(0, 3)
     def _(i):
         first_product(0, (5 - i) % 4)
+
+    node_ids = lax.broadcasted_iota(jnp.int32, (G, S), 0)
+    weight[...] = jnp.where(node_ids == node_ref[...], prob_ref[...], 0.0).astype(bf16)
+    mass_s[0] = nt(jnp.ones((16, S), bf16), weight[...])[0:8]
+    mass_twin = send(mass_s.at[0], mass_r.at[0], m_send, m_recv, 0, twin)
 
     a1[0].wait_recv()
     a1[1].wait_recv()
@@ -171,12 +178,9 @@
                 send(b2_s.at[1], b2_r.at[1], rs_send, rs_recv, 11, left),
             ]
 
-    node_ids = lax.broadcasted_iota(jnp.int32, (G, S), 0)
-    same = node_ids == node_ref[...]
-    member[...] = jnp.where(same, 1.0, 0.0).astype(bf16)
-    weight[...] = jnp.where(same, prob_ref[...], 0.0).astype(bf16)
-    mass_s[...] = nt(jnp.ones((16, S), bf16), weight[...])[0:8]
-    mass_twin = send(mass_s, mass_r, m_send, m_recv, 0, twin)
+    mass_twin.wait_recv()
+    mass_s[1] = mass_s[0] + mass_r[0]
+    mass_over = send(mass_s.at[1], mass_r.at[1], m_send, m_recv, 1, over)
     for copy in others:
         copy.wait()
 
@@ -202,11 +206,11 @@
     ).astype(bf16)
     a3 = send(a3_s, a3_r, rs_send, rs_recv, 14, across)
 
-    mass_twin.wait_recv()
-    mass_c[...] = mass_s[...] + mass_r[...]
-    mass_copies = [
-        send(mass_c, mass_p.at[k], m_send, m_recv, 1 + k, peer(oy, oz))
-        for k, (oy, oz) in enumerate(offsets)
+    mass_over.wait_recv()
+    mass_s[2] = mass_s[1] + mass_r[1]
+    mass_z = [
+        send(mass_s.at[2], mass_r.at[2], m_send, m_recv, 2, up),
+        send(mass_s.at[2], mass_r.at[3], m_send, m_recv, 3, down),
     ]
 
     demand_t = demand_v[...].T
@@ -306,12 +310,13 @@
     rec_own[...] = nt(kkt_v[...], rhs[...]).astype(bf16)
     write_rec = pltpu.make_async_copy(rec_own, recourse_out, out_sem.at[0])
     write_rec.start()
+    mass_z[0].wait_recv()
+    mass_z[1].wait_recv()
+    mass_z.append(send(mass_s.at[2], mass_r.at[4], m_send, m_recv, 4, peer(0, 2)))
     turn_2()
     rest_2()
     end_high_2()
     end_low_2()
-
-    CH = 128
 
     def plan(rows):
         linked = nt(tech_v[rows, :], rec[...])
@@ -321,95 +326,129 @@
         return nt(planned, weight[...])
 
     def core_copy(j):
-        rows = pl.ds(pl.multiple_of(j * CH, CH), CH)
         return pltpu.make_async_remote_copy(
-            src_ref=e1_s.at[rows], dst_ref=e1_r.at[rows],
+            src_ref=e1_s.at[j], dst_ref=e1_r.at[j],
             send_sem=e1_send.at[j], recv_sem=e1_recv.at[j],
             device_id=twin, device_id_type=MESH,
         )
 
-    @pl.loop(0, HALF // CH)
+    def slice_copy(oy, oz):
+        k = oz * 2 + oy
+        rows = pl.ds(pl.multiple_of(((yh + oy) % 2) * SLICE, SLICE), SLICE)
+        return pltpu.make_async_remote_copy(
+            src_ref=e2_s.at[oz, rows], dst_ref=e2_r.at[k],
+            send_sem=e2_send.at[k], recv_sem=e2_recv.at[k],
+            device_id=peer(oy, oz), device_id_type=MESH,
+        )
+
+    def core_rows(c):
+        return pl.ds(pl.multiple_of(c * (CH // 2), CH // 2), CH // 2)
+
+    def join(oz):
+        core_copy(oz).wait_recv()
+        total = tot[oz, core_rows(core), :] + e1_r[oz].astype(f32)
+        tot[oz, core_rows(core), :] = total
+        e2_s[oz] = total.astype(bf16)
+
+    def compute(oz):
+        tot[oz] = plan(pl.ds(pl.multiple_of(((z + oz) % 4) * CH, CH), CH))
+        e1_s[oz] = tot[oz, core_rows(1 - core), :].astype(bf16)
+        core_copy(oz).start()
+
+    compute(3)
+
+    @pl.loop(0, 3)
     def _(j):
-        rows = pl.ds(pl.multiple_of((1 - core) * HALF + j * CH, CH), CH)
-        e1_s[pl.ds(pl.multiple_of(j * CH, CH), CH), :] = plan(rows).astype(bf16)
-        core_copy(j).start()
-
-    @pl.loop(0, HALF // CH)
-    def _(j):
-        rows = pl.ds(pl.multiple_of(core * HALF + j * CH, CH), CH)
-        here = pl.ds(pl.multiple_of(j * CH, CH), CH)
-        mine = plan(rows)
-        core_copy(j).wait_recv()
-        total = mine + e1_r[here, :].astype(f32)
-        tot[here, :] = total
-        e2_s[here, :] = total.astype(bf16)
-
-    def slice_of(p):
-        return pl.ds(pl.multiple_of(p * SLICE, SLICE), SLICE)
-
-    e2 = [
-        send(e2_s.at[slice_of(peer_id(oy, oz))], e2_r.at[k], e2_send, e2_recv, k, peer(oy, oz))
-        for k, (oy, oz) in enumerate(offsets)
-    ]
+        compute(2 - j)
+        join(3 - j)
+        slice_copy(0, 3 - j).start()
+        slice_copy(1, 3 - j).start()
+
+    join(0)
+    slice_copy(1, 0).start()
     write_planned = pltpu.make_async_copy(planned_v, planned_out, out_sem.at[1])
     write_planned.start()
-    me = peer_id(0, 0)
-    mass = mass_c[...]
-    for k in range(7):
-        mass_copies[k].wait_recv()
-        mass = mass + mass_p[k]
-    total = tot[slice_of(me), :]
-    for k in range(7):
-        e2[k].wait_recv()
-        total = total + e2_r[k].astype(f32)
-
-    def cons_at(c, p):
-        return pl.ds(pl.multiple_of(c * HALF + p * SLICE, SLICE), SLICE)
-
-    mine = cons_at(core, me)
+    mass_z[2].wait_recv()
+    mass = mass_s[2] + mass_r[2] + mass_r[3] + mass_r[4]
+    total = tot[0, pl.ds(pl.multiple_of(core * (CH // 2) + yh * SLICE, SLICE), SLICE), :]
+    for oy, oz in ((0, 3), (1, 3), (0, 2), (1, 2), (0, 1), (1, 1), (1, 0)):
+        slice_copy(oy, oz).wait_recv()
+        total = total + e2_r[oz * 2 + oy].astype(f32)
+
+    def cons_at(oy, oz):
+        first = ((z + oz) % 4) * CH + core * (CH // 2) + ((yh + oy) % 2) * SLICE
+        return pl.ds(pl.multiple_of(first, SLICE), SLICE)
+
+    mine = cons_at(0, 0)
     cons_b[mine, :] = (total / mass[0:1, :]).astype(bf16)
     f = [
         send(cons_b.at[mine], cons_b.at[mine], f_send, f_recv, k, peer(oy, oz))
         for k, (oy, oz) in enumerate(offsets)
     ]
     c = [send(cons_b.at[mine], cons_b.at[mine], c_send, c_recv, 7, twin)]
-    for k, (oy, oz) in enumerate(offsets):
+    for k, (oy, oz) in reversed(list(enumerate(offsets))):
         f[k].wait_recv()
-        theirs = cons_at(core, peer_id(oy, 4 - oz))
+        theirs = cons_at(oy, 4 - oz)
         c.append(send(cons_b.at[theirs], cons_b.at[theirs], c_send, c_recv, k, twin))
-
-    def finish(which):
-        @pl.loop(0, HALF // CH)
-        def _(j):
-            rows = pl.ds(pl.multiple_of(which * HALF + j * CH, CH), CH)
-            spread = nn(cons_b[rows, :], member[...])
-            cons_f[rows, :] = cons_b[rows, :].astype(f32)
-            mult_v[rows, :] = mult_v[rows, :] + PENALTY * (planned_v[rows, :].astype(f32) - spread)
-
-        both = pl.ds(pl.multiple_of(which * HALF, HALF), HALF)
-        return both
-
-    writes = []
-
-    def put(both, k):
-        writes.append(pltpu.make_async_copy(cons_f.at[both], cons_out.at[both], out_sem.at[2 + k]))
-        writes.append(pltpu.make_async_copy(mult_v.at[both], next_out.at[both], out_sem.at[4 + k]))
-        writes[-1].start()
-        writes[-2].start()
-
-    put(finish(core), 0)
     for copy in c:
         copy.wait_recv()
-    put(finish(1 - core), 1)
+    write_cons = pltpu.make_async_copy(cons_b, cons_out, out_sem.at[2])
+    write_cons.start()
 
     for copy in started:
         copy.wait_send()
-    for j in range(HALF // CH):
-        core_copy(j).wait_send()
+    for oz in range(4):
+        core_copy(oz).wait_send()
+        for oy in range(2):
+            if oz or oy:
+                slice_copy(oy, oz).wait_send()
     write_rec.wait()
     write_planned.wait()
+    write_cons.wait()
+
+
+def last_kernel(
+    planned_hbm, recourse_hbm, cons_hbm, mult_hbm, node_ref,
+    planned_out, recourse_out, cons_out, next_out,
+    planned_v, recourse_v, cons_v, mult_v, cons_f, member, load, out_sem,
+):
+    pairs = ((planned_hbm, planned_v), (recourse_hbm, recourse_v), (cons_hbm, cons_v))
+    loads = [pltpu.make_async_copy(a, b, load.at[k]) for k, (a, b) in enumerate(pairs)]
+    loads.append(pltpu.make_async_copy(mult_hbm, mult_v, load.at[3]))
+    for copy in loads:
+        copy.start()
+    node_ids = lax.broadcasted_iota(jnp.int32, (G, S), 0)
+    member[...] = jnp.where(node_ids == node_ref[...], 1.0, 0.0).astype(bf16)
+    loads[0].wait()
+    writes = [pltpu.make_async_copy(planned_v, planned_out, out_sem.at[0])]
+    writes[0].start()
+    loads[1].wait()
+    writes.append(pltpu.make_async_copy(recourse_v, recourse_out, out_sem.at[1]))
+    writes[1].start()
+    loads[2].wait()
+    loads[3].wait()
+
+    def put(j):
+        rows = pl.ds(pl.multiple_of(j * CH, CH), CH)
+        return (
+            pltpu.make_async_copy(cons_f.at[rows], cons_out.at[rows], out_sem.at[2 + j]),
+            pltpu.make_async_copy(mult_v.at[rows], next_out.at[rows], out_sem.at[6 + j]),
+        )
+
+    @pl.loop(0, ROWS // CH)
+    def _(j):
+        rows = pl.ds(pl.multiple_of(j * CH, CH), CH)
+        spread = nn(cons_v[rows, :], member[...])
+        cons_f[rows, :] = cons_v[rows, :].astype(f32)
+        mult_v[rows, :] = mult_v[rows, :] + PENALTY * (planned_v[rows, :].astype(f32) - spread)
+        for copy in put(j):
+            copy.start()
+
     for copy in writes:
         copy.wait()
+    for j in range(ROWS // CH):
+        for copy in put(j):
+            copy.wait()
 
 
 def on_device(
@@ -417,6 +456,7 @@
 ):
     any_space = pl.BlockSpec(memory_space=pl.ANY)
     vmem = pl.BlockSpec(memory_space=pltpu.VMEM)
+    hbm = pl.BlockSpec(memory_space=pltpu.HBM)
     V = pltpu.VMEM
     D = pltpu.SemaphoreType.DMA
     scratch = [
@@ -430,33 +470,49 @@
         V((2, HB, B), bf16), V((2, HB, B), bf16),
         V((2, RB, B), bf16), V((2, RB, B), bf16),
         V((S, M), bf16), V((S, M), bf16), V((B, S), bf16),
-        V((G, S), bf16), V((G, S), bf16),
-        V((8, G), f32), V((8, G), f32), V((8, G), f32), V((7, 8, G), f32),
-        V((ROWS, S), bf16), V((HALF, G), f32), V((HALF, G), bf16), V((HALF, G), bf16),
-        V((HALF, G), bf16), V((7, SLICE, G), bf16), V((ROWS, G), bf16), V((ROWS, G), f32),
-        D((5,)), D((8,)), D((6,)),
+        V((G, S), bf16), V((3, 8, G), f32), V((5, 8, G), f32),
+        V((ROWS, S), bf16), V((4, CH, G), f32),
+        V((4, CH // 2, G), bf16), V((4, CH // 2, G), bf16),
+        V((4, CH // 2, G), bf16), V((8, SLICE, G), bf16), V((ROWS, G), bf16),
+        D((5,)), D((8,)), D((3,)),
         D((15,)), D((15,)), D((18,)), D((18,)), D((18,)), D((18,)),
-        D((8,)), D((8,)), D((4,)), D((4,)), D((7,)), D((7,)), D((7,)), D((7,)), D((8,)), D((8,)),
+        D((5,)), D((5,)), D((4,)), D((4,)), D((8,)), D((8,)), D((7,)), D((7,)), D((8,)), D((8,)),
     ]
+    node_row = scenario_node.reshape(1, S)
+    planned, recourse, consensus = pl.pallas_call(
+        kernel,
+        out_shape=(
+            jax.ShapeDtypeStruct((ROWS, S), bf16),
+            jax.ShapeDtypeStruct((B, S), bf16),
+            jax.ShapeDtypeStruct((ROWS, G), bf16),
+        ),
+        in_specs=[any_space] * 6 + [vmem] * 2,
+        out_specs=(any_space,) * 3,
+        scratch_shapes=scratch,
+        compiler_params=pltpu.CompilerParams(
+            collective_id=0, has_side_effects=True, vmem_limit_bytes=56 * 2**20
+        ),
+    )(
+        order_qty, multiplier, unit_cost, demand, technology, kkt_inverse,
+        probability.reshape(1, S), node_row,
+    )
     return tuple(
         pl.pallas_call(
-            kernel,
+            last_kernel,
             out_shape=(
                 jax.ShapeDtypeStruct((ROWS, S), bf16),
                 jax.ShapeDtypeStruct((B, S), bf16),
                 jax.ShapeDtypeStruct((ROWS, G), f32),
                 jax.ShapeDtypeStruct((ROWS, S), f32),
             ),
-            in_specs=[any_space] * 6 + [vmem] * 2,
+            in_specs=[hbm] * 4 + [vmem],
             out_specs=(any_space,) * 4,
-            scratch_shapes=scratch,
-            compiler_params=pltpu.CompilerParams(
-                collective_id=0, has_side_effects=True, vmem_limit_bytes=56 * 2**20
-            ),
-        )(
-            order_qty, multiplier, unit_cost, demand, technology, kkt_inverse,
-            probability.reshape(1, S), scenario_node.reshape(1, S),
-        )
+            scratch_shapes=[
+                V((ROWS, S), bf16), V((B, S), bf16), V((ROWS, G), bf16), V((ROWS, S), f32),
+                V((ROWS, G), f32), V((G, S), bf16), D((4,)), D((10,)),
+            ],
+            compiler_params=pltpu.CompilerParams(vmem_limit_bytes=32 * 2**20),
+        )(planned, recourse, consensus, multiplier, node_row)
     )
 
 

time: 94.7 us -> 89.1 us (0.941)
  local copies, waits for them, and re-layouts: 7.75 us -> 3.4 us
  Pallas kernels: 86.1 us -> 84.8 us
    unnamed x8 -> x10, local copies, waits for them, and re-layouts: 7.75 us -> 3.4 us
    pallas_call x1, Pallas kernels: 86.1 us -> 81.8 us  [on_device(): pl.pallas_call(kernel, out_shape=(jax.ShapeDtypeStruct((ROWS, S), bf16),...]
    pallas_call x0 -> x1, Pallas kernels: none -> 2.93 us  [on_device(): pl.pallas_call(last_kernel, out_shape=(jax.ShapeDtypeStruct((ROWS, S), bf...]
where the time goes in v2:
time: 89.1 us; the launch traced here: 88.8 us
  Pallas kernels  84.8 us (95%)
  local copies, waits for them, and re-layouts  3.4 us (4%)
    pallas_call x1, Pallas kernels, on_device(): pl.pallas_call(kernel, out_shape=(jax.ShapeDtypeStruct((ROWS, S), bf16),...  81.8 us
    unnamed x10, local copies, waits for them, and re-layouts  3.4 us
    pallas_call x1, Pallas kernels, on_device(): pl.pallas_call(last_kernel, out_shape=(jax.ShapeDtypeStruct((ROWS, S), bf...  2.93 us

profile of v2, /device:TPU:1, one launch (start us, length us, event | category | flops | bytes accessed | tf_op | source)
XLA Modules:
  0.0 88.8 jit_solution(3212056577122902968)
XLA Ops:
  0.6 0.0 copy-start
  0.6 0.0 copy-start.4
  0.7 81.8 %shard_map.111 = (bf16[1024,512]{1,0:T(8,128)(2,1)}, bf16[256,512]{1,0:T(8,128)(2,1)}, bf16[1024,512]{1,0:T(8,128)(2,1)}) custom-call(bf16[1024,512]{1,0:T(8,128)(2,1)} %order_hbm.1, f32[1024,512]{1,0:T(8,128)} %mult_hbm.3, bf16[1024,512]{1,0:T(8,128)(2,1)} %cost_hbm.1, bf16[256,512]{1,0:T(8,128)(2,1)} %demand_hbm.1, bf16[1024,2048]{1,0:T(8,128)(2,1)} %tech_hbm.1, ...), custom_call_target="tpu_custom_call" | custom-call | tf_op jit(solution)/shard_map/pallas_call | solution.py:482
  82.5 0.0 copy-done
  82.5 0.0 copy-done.4
  82.5 0.0 copy-start.1
  82.5 1.2 %copy-done.1 = bf16[1024,512]{1,0:T(8,128)(2,1)S(1)} copy-done((bf16[1024,512]{1,0:T(8,128)(2,1)S(1)}, bf16[1024,512]{1,0:T(8,128)(2,1)}, u32[]{:S(2)}) %copy-start.1) | copy-done | bytes 1048600
  83.7 0.0 copy-start.2
  83.7 1.2 %copy-done.2 = bf16[1024,512]{1,0:T(8,128)(2,1)S(1)} copy-done((bf16[1024,512]{1,0:T(8,128)(2,1)S(1)}, bf16[1024,512]{1,0:T(8,128)(2,1)}, u32[]{:S(2)}) %copy-start.2) | copy-done | bytes 1048600
  85.0 0.0 copy-start.3
  85.0 0.9 %copy-done.3 = bf16[256,512]{1,0:T(8,128)(2,1)S(1)} copy-done((bf16[256,512]{1,0:T(8,128)(2,1)S(1)}, bf16[256,512]{1,0:T(8,128)(2,1)}, u32[]{:S(2)}) %copy-start.3) | copy-done | bytes 262168
  85.9 2.9 %shard_map.112 = (bf16[1024,512]{1,0:T(8,128)(2,1)}, bf16[256,512]{1,0:T(8,128)(2,1)}, f32[1024,512]{1,0:T(8,128)}, f32[1024,512]{1,0:T(8,128)}) custom-call(bf16[1024,512]{1,0:T(8,128)(2,1)S(1)} %copy-done.1, bf16[256,512]{1,0:T(8,128)(2,1)S(1)} %copy-done.3, bf16[1024,512]{1,0:T(8,128)(2,1)S(1)} %copy-done.2, f32[1024,512]{1,0:T(8,128)S(1)} %copy-done, ...), custom_call_target="tpu_custom_call" | custom-call | tf_op jit(solution)/shard_map/pallas_call | solution.py:500
Async XLA Ops:
  0.6 81.9 %copy-start = (f32[1024,512]{1,0:T(8,128)S(1)}, f32[1024,512]{1,0:T(8,128)}, u32[]{:S(2)}) copy-start(f32[1024,512]{1,0:T(8,128)} %mult_hbm.3) | copy-start | bytes 6291460
  0.6 81.9 %copy-start.4 = (s32[512,1]{0,1:T(1,128)S(1)}, s32[512,1]{0,1:T(1,128)}, u32[]{:S(2)}) copy-start(s32[512,1]{0,1:T(1,128)} %param.15) | copy-start | bytes 6148
  82.5 1.2 %copy-start.1 = (bf16[1024,512]{1,0:T(8,128)(2,1)S(1)}, bf16[1024,512]{1,0:T(8,128)(2,1)}, u32[]{:S(2)}) copy-start(bf16[1024,512]{1,0:T(8,128)(2,1)} %get-tuple-element.7.planned_hbm) | copy-start | bytes 3145732
  83.7 1.2 %copy-start.2 = (bf16[1024,512]{1,0:T(8,128)(2,1)S(1)}, bf16[1024,512]{1,0:T(8,128)(2,1)}, u32[]{:S(2)}) copy-start(bf16[1024,512]{1,0:T(8,128)(2,1)} %get-tuple-element.9.cons_hbm) | copy-start | bytes 3145732
  85.0 0.9 %copy-start.3 = (bf16[256,512]{1,0:T(8,128)(2,1)S(1)}, bf16[256,512]{1,0:T(8,128)(2,1)}, u32[]{:S(2)}) copy-start(bf16[256,512]{1,0:T(8,128)(2,1)} %get-tuple-element.8.recourse_hbm) | copy-start | bytes 786436

commit v3 on v2

--- a/solution.py
+++ b/solution.py
@@ -15,6 +15,7 @@
 B = 256
 SLICE = 64
 CH = 256
+PIECE = M // 16
 
 RA = 288
 HA = RA // 2
@@ -41,11 +42,11 @@
     part,
     a1_s, a1_r, a2_s, a2_r, a3_s, a3_r,
     b1_s, b1_r, b2_s, b2_r, b3_s, b3_r,
-    rhs, rec, rec_own,
+    rhs, link, kkt_cols, rec_own,
     weight, mass_s, mass_r,
     planned_v, tot, e1_s, e1_r, e2_s, e2_r, cons_b,
     load, tload, out_sem,
-    rs_send, rs_recv, ag1_send, ag1_recv, ag2_send, ag2_recv,
+    rs_send, rs_recv, ag1_send, ag1_recv, k_send, k_recv, l_send, l_recv, t_send, t_recv,
     m_send, m_recv, e1_send, e1_recv, e2_send, e2_recv, f_send, f_recv, c_send, c_recv,
 ):
     s = lax.axis_index("scen")
@@ -85,6 +86,12 @@
         started.append(copy)
         return copy
 
+    piece = pl.ds(pl.multiple_of(s * PIECE, PIECE), PIECE)
+    kkt_rows = pl.ds(pl.multiple_of(d * B, B), B)
+    load_piece = pltpu.make_async_copy(
+        kkt_hbm.at[:, piece], kkt_cols.at[kkt_rows, :], load.at[5]
+    )
+    load_piece.start()
     load_order = pltpu.make_async_copy(order_hbm, order_v, load.at[0])
     load_order.start()
 
@@ -130,6 +137,18 @@
 
     pl.semaphore_wait(barrier, len(everyone))
 
+    def kkt_send(dx, dy, part_of, target, k):
+        first, size = part_of
+        e = pl.ds(pl.multiple_of(dec_id(dx, dy) * B + first, B // 2), size)
+        return send(kkt_cols.at[e, :], kkt_cols.at[e, :], k_send, k_recv, k, target)
+
+    whole, half0, half1 = (0, B), (0, B // 2), (B // 2, B // 2)
+    load_piece.wait()
+    kc = [
+        kkt_send(0, 0, whole, across, 0),
+        kkt_send(0, 0, whole, right, 1),
+        kkt_send(0, 0, whole, left, 2),
+    ]
     a1 = [
         send(a1_s.at[0], a1_r.at[0], rs_send, rs_recv, 0, right),
         send(a1_s.at[1], a1_r.at[1], rs_send, rs_recv, 1, left),
@@ -149,10 +168,18 @@
 
     for r in range(5, 8):
         tech_copy(r).wait()
+    kc[0].wait_recv()
+    kc.append(kkt_send(0, 1, whole, right, 3))
+    kc.append(kkt_send(0, 1, whole, left, 4))
 
     @pl.loop(0, 3)
     def _(i):
         first_product(0, (5 - i) % 4)
+
+    kc[1].wait_recv()
+    kc.append(kkt_send(3, 0, half0, right, 5))
+    kc[2].wait_recv()
+    kc.append(kkt_send(1, 0, half1, left, 6))
 
     node_ids = lax.broadcasted_iota(jnp.int32, (G, S), 0)
     weight[...] = jnp.where(node_ids == node_ref[...], prob_ref[...], 0.0).astype(bf16)
@@ -181,6 +208,10 @@
     mass_twin.wait_recv()
     mass_s[1] = mass_s[0] + mass_r[0]
     mass_over = send(mass_s.at[1], mass_r.at[1], m_send, m_recv, 1, over)
+    kc[3].wait_recv()
+    kc.append(kkt_send(3, 1, half0, right, 7))
+    kc[4].wait_recv()
+    kc.append(kkt_send(1, 1, half1, left, 8))
     for copy in others:
         copy.wait()
 
@@ -212,6 +243,36 @@
         send(mass_s.at[2], mass_r.at[2], m_send, m_recv, 2, up),
         send(mass_s.at[2], mass_r.at[3], m_send, m_recv, 3, down),
     ]
+
+    for k in range(5, 9):
+        kc[k].wait_recv()
+
+    @pl.loop(0, ROWS // CH)
+    def _(j):
+        rows = pl.ds(pl.multiple_of(j * CH, CH), CH)
+        link[rows, piece] = nn(tech_v[rows, :], kkt_cols[...]).astype(bf16)
+
+    def link_piece(oy, oz):
+        return pl.ds(pl.multiple_of((peer_id(oy, oz) * 2 + core) * PIECE, PIECE), PIECE)
+
+    def link_send(oy, oz, target, k):
+        where = link.at[:, link_piece(oy, oz)]
+        return send(where, where, l_send, l_recv, k, target)
+
+    def twin_send(oy, oz, k):
+        where = link.at[:, link_piece(oy, oz)]
+        return send(where, where, t_send, t_recv, k, twin)
+
+    mass_z[0].wait_recv()
+    mass_z[1].wait_recv()
+    mass_z.append(send(mass_s.at[2], mass_r.at[4], m_send, m_recv, 4, peer(0, 2)))
+    lc = [
+        link_send(0, 0, over, 0),
+        link_send(0, 0, up, 1),
+        link_send(0, 0, down, 2),
+        link_send(0, 0, peer(0, 2), 3),
+    ]
+    tc = [twin_send(0, 0, 0)]
 
     demand_t = demand_v[...].T
     own = pl.ds(pl.multiple_of(d * B, B), B)
@@ -285,7 +346,6 @@
         return start_high, start_low, first_turn, rest, end_high, end_low
 
     high_1, low_1, turn_1, rest_1, end_high_1, end_low_1 = gatherer(rhs, ag1_send, ag1_recv)
-    high_2, low_2, turn_2, rest_2, end_high_2, end_low_2 = gatherer(rec, ag2_send, ag2_recv)
 
     high_1()
     a2[0, 0].wait_recv()
@@ -299,27 +359,26 @@
         )
     ).astype(bf16)
     low_1()
+    lc[0].wait_recv()
+    lc.append(link_send(1, 0, up, 4))
+    lc.append(link_send(1, 0, down, 5))
+    lc.append(link_send(1, 0, peer(0, 2), 6))
+    tc.append(twin_send(1, 0, 1))
     turn_1()
     rest_1()
+    for k, oz in ((1, 3), (2, 1), (3, 2)):
+        lc[k].wait_recv()
+        tc.append(twin_send(0, oz, 1 + k))
     end_high_1()
-    rec[RA:S, own] = nt(rhs[RA:S], kkt_v[...]).astype(bf16)
-    high_2()
     end_low_1()
-    rec[0:RA, own] = nt(rhs[0:RA], kkt_v[...]).astype(bf16)
-    low_2()
-    rec_own[...] = nt(kkt_v[...], rhs[...]).astype(bf16)
-    write_rec = pltpu.make_async_copy(rec_own, recourse_out, out_sem.at[0])
-    write_rec.start()
-    mass_z[0].wait_recv()
-    mass_z[1].wait_recv()
-    mass_z.append(send(mass_s.at[2], mass_r.at[4], m_send, m_recv, 4, peer(0, 2)))
-    turn_2()
-    rest_2()
-    end_high_2()
-    end_low_2()
+    for k, oz in ((4, 3), (5, 1), (6, 2)):
+        lc[k].wait_recv()
+        tc.append(twin_send(1, oz, 1 + k))
+    for copy in tc:
+        copy.wait_recv()
 
     def plan(rows):
-        linked = nt(tech_v[rows, :], rec[...])
+        linked = nt(link[rows, :], rhs[...])
         gradient = cost_v[rows, :].astype(f32) + mult_v[rows, :] + linked
         planned = jnp.maximum(order_v[rows, :].astype(f32) - STEP * gradient, 0.0).astype(bf16)
         planned_v[rows, :] = planned
@@ -368,6 +427,9 @@
     slice_copy(1, 0).start()
     write_planned = pltpu.make_async_copy(planned_v, planned_out, out_sem.at[1])
     write_planned.start()
+    rec_own[...] = nt(kkt_v[...], rhs[...]).astype(bf16)
+    write_rec = pltpu.make_async_copy(rec_own, recourse_out, out_sem.at[0])
+    write_rec.start()
     mass_z[2].wait_recv()
     mass = mass_s[2] + mass_r[2] + mass_r[3] + mass_r[4]
     total = tot[0, pl.ds(pl.multiple_of(core * (CH // 2) + yh * SLICE, SLICE), SLICE), :]
@@ -469,13 +531,13 @@
         V((4, RB, B), bf16), V((4, RB, B), bf16),
         V((2, HB, B), bf16), V((2, HB, B), bf16),
         V((2, RB, B), bf16), V((2, RB, B), bf16),
-        V((S, M), bf16), V((S, M), bf16), V((B, S), bf16),
+        V((S, M), bf16), V((ROWS, M), bf16), V((M, PIECE), bf16), V((B, S), bf16),
         V((G, S), bf16), V((3, 8, G), f32), V((5, 8, G), f32),
         V((ROWS, S), bf16), V((4, CH, G), f32),
         V((4, CH // 2, G), bf16), V((4, CH // 2, G), bf16),
         V((4, CH // 2, G), bf16), V((8, SLICE, G), bf16), V((ROWS, G), bf16),
-        D((5,)), D((8,)), D((3,)),
-        D((15,)), D((15,)), D((18,)), D((18,)), D((18,)), D((18,)),
+        D((6,)), D((8,)), D((3,)),
+        D((15,)), D((15,)), D((18,)), D((18,)), D((9,)), D((9,)), D((7,)), D((7,)), D((8,)), D((8,)),
         D((5,)), D((5,)), D((4,)), D((4,)), D((8,)), D((8,)), D((7,)), D((7,)), D((8,)), D((8,)),
     ]
     node_row = scenario_node.reshape(1, S)
@@ -511,7 +573,7 @@
                 V((ROWS, S), bf16), V((B, S), bf16), V((ROWS, G), bf16), V((ROWS, S), f32),
                 V((ROWS, G), f32), V((G, S), bf16), D((4,)), D((10,)),
             ],
-            compiler_params=pltpu.CompilerParams(vmem_limit_bytes=32 * 2**20),
+            compiler_params=pltpu.CompilerParams(vmem_limit_bytes=60 * 2**20),
         )(planned, recourse, consensus, multiplier, node_row)
     )
 

time: 89.1 us -> 84 us (0.943)
  local copies, waits for them, and re-layouts: 3.4 us -> 0 us
  Pallas kernels: 84.8 us -> 83.2 us
    pallas_call x1, Pallas kernels: 81.8 us -> 77.6 us  [on_device(): pl.pallas_call(kernel, out_shape=(jax.ShapeDtypeStruct((ROWS, S), bf16),...]
    unnamed x10 -> x0, local copies, waits for them, and re-layouts: 3.4 us -> none
    pallas_call x1, Pallas kernels: 2.93 us -> 5.51 us  [on_device(): pl.pallas_call(last_kernel, out_shape=(jax.ShapeDtypeStruct((ROWS, S), bf...]
where the time goes in v3:
time: 84 us; the launch traced here: 83.8 us
  Pallas kernels  83.2 us (99%)
    pallas_call x1, Pallas kernels, on_device(): pl.pallas_call(kernel, out_shape=(jax.ShapeDtypeStruct((ROWS, S), bf16),...  77.6 us
    pallas_call x1, Pallas kernels, on_device(): pl.pallas_call(last_kernel, out_shape=(jax.ShapeDtypeStruct((ROWS, S), bf...  5.51 us

profile of v3, /device:TPU:1, one launch (start us, length us, event | category | flops | bytes accessed | tf_op | source)
XLA Modules:
  0.0 83.8 jit_solution(14947772731540099029)
XLA Ops:
  0.6 77.6 %shard_map.111 = (bf16[1024,512]{1,0:T(8,128)(2,1)}, bf16[256,512]{1,0:T(8,128)(2,1)}, bf16[1024,512]{1,0:T(8,128)(2,1)}) custom-call(bf16[1024,512]{1,0:T(8,128)(2,1)} %order_hbm.1, f32[1024,512]{1,0:T(8,128)} %mult_hbm.3, bf16[1024,512]{1,0:T(8,128)(2,1)} %cost_hbm.1, bf16[256,512]{1,0:T(8,128)(2,1)} %demand_hbm.1, bf16[1024,2048]{1,0:T(8,128)(2,1)} %tech_hbm.1, ...), custom_call_target="tpu_custom_call" | custom-call | tf_op jit(solution)/shard_map/pallas_call | solution.py:544
  78.3 5.5 %shard_map.112 = (bf16[1024,512]{1,0:T(8,128)(2,1)}, bf16[256,512]{1,0:T(8,128)(2,1)}, f32[1024,512]{1,0:T(8,128)}, f32[1024,512]{1,0:T(8,128)}) custom-call(bf16[1024,512]{1,0:T(8,128)(2,1)} %get-tuple-element.7.planned_hbm, bf16[256,512]{1,0:T(8,128)(2,1)} %get-tuple-element.8.recourse_hbm, bf16[1024,512]{1,0:T(8,128)(2,1)} %get-tuple-element.9.cons_hbm, ...), custom_call_target="tpu_custom_call" | custom-call | tf_op jit(solution)/shard_map/pallas_call | solution.py:562

commit v4 on v3

--- a/solution.py
+++ b/solution.py
@@ -37,15 +37,15 @@
 
 def kernel(
     order_hbm, mult_hbm, cost_hbm, demand_hbm, tech_hbm, kkt_hbm, prob_ref, node_ref,
-    planned_out, recourse_out, cons_out,
+    planned_v, rec_own, cons_out,
     order_v, order_t, mult_v, cost_v, demand_v, tech_v, kkt_v,
     part,
     a1_s, a1_r, a2_s, a2_r, a3_s, a3_r,
     b1_s, b1_r, b2_s, b2_r, b3_s, b3_r,
-    rhs, link, kkt_cols, rec_own,
+    rhs, link, kkt_cols,
     weight, mass_s, mass_r,
-    planned_v, tot, e1_s, e1_r, e2_s, e2_r, cons_b,
-    load, tload, out_sem,
+    tot, e1_s, e1_r, e2_s, e2_r, cons_b,
+    load, tload,
     rs_send, rs_recv, ag1_send, ag1_recv, k_send, k_recv, l_send, l_recv, t_send, t_recv,
     m_send, m_recv, e1_send, e1_recv, e2_send, e2_recv, f_send, f_recv, c_send, c_recv,
 ):
@@ -71,7 +71,8 @@
     up, down, over = peer(0, 1), peer(0, 3), peer(1, 0)
 
     barrier = pltpu.get_barrier_semaphore()
-    everyone = [right, left, across, twin, up, down, over]
+    beyond = (s, dec_id(2, 0))
+    everyone = [right, left, across, twin, up, down, over, beyond]
     for other in everyone:
         pl.semaphore_signal(barrier, inc=1, device_id=other, device_id_type=MESH)
 
@@ -116,6 +117,9 @@
     for copy in others:
         copy.start()
 
+    node_ids = lax.broadcasted_iota(jnp.int32, (G, S), 0)
+    weight[...] = jnp.where(node_ids == node_ref[...], prob_ref[...], 0.0).astype(bf16)
+    mass_s[0] = nt(jnp.ones((16, S), bf16), weight[...])[0:8]
     load_order.wait()
     order_t[...] = order_v[...].T
 
@@ -137,24 +141,19 @@
 
     pl.semaphore_wait(barrier, len(everyone))
 
-    def kkt_send(dx, dy, part_of, target, k):
-        first, size = part_of
-        e = pl.ds(pl.multiple_of(dec_id(dx, dy) * B + first, B // 2), size)
+    def kkt_send(dy, target, k):
+        e = pl.ds(pl.multiple_of(dec_id(0, dy) * B, B), B)
         return send(kkt_cols.at[e, :], kkt_cols.at[e, :], k_send, k_recv, k, target)
 
-    whole, half0, half1 = (0, B), (0, B // 2), (B // 2, B // 2)
     load_piece.wait()
-    kc = [
-        kkt_send(0, 0, whole, across, 0),
-        kkt_send(0, 0, whole, right, 1),
-        kkt_send(0, 0, whole, left, 2),
-    ]
+    kc = [kkt_send(0, to, k) for k, to in enumerate((across, right, left, beyond))]
     a1 = [
         send(a1_s.at[0], a1_r.at[0], rs_send, rs_recv, 0, right),
         send(a1_s.at[1], a1_r.at[1], rs_send, rs_recv, 1, left),
     ]
     b1 = {2: send(b1_s.at[2], b1_r.at[2], rs_send, rs_recv, 2, across)}
 
+    mass_twin = send(mass_s.at[0], mass_r.at[0], m_send, m_recv, 0, twin)
     for r in range(2, 5):
         tech_copy(r).wait()
 
@@ -169,22 +168,15 @@
     for r in range(5, 8):
         tech_copy(r).wait()
     kc[0].wait_recv()
-    kc.append(kkt_send(0, 1, whole, right, 3))
-    kc.append(kkt_send(0, 1, whole, left, 4))
+    for k, to in ((4, right), (5, left), (6, beyond)):
+        kc.append(kkt_send(1, to, k))
+    mass_twin.wait_recv()
+    mass_s[1] = mass_s[0] + mass_r[0]
+    mass_over = send(mass_s.at[1], mass_r.at[1], m_send, m_recv, 1, over)
 
     @pl.loop(0, 3)
     def _(i):
         first_product(0, (5 - i) % 4)
-
-    kc[1].wait_recv()
-    kc.append(kkt_send(3, 0, half0, right, 5))
-    kc[2].wait_recv()
-    kc.append(kkt_send(1, 0, half1, left, 6))
-
-    node_ids = lax.broadcasted_iota(jnp.int32, (G, S), 0)
-    weight[...] = jnp.where(node_ids == node_ref[...], prob_ref[...], 0.0).astype(bf16)
-    mass_s[0] = nt(jnp.ones((16, S), bf16), weight[...])[0:8]
-    mass_twin = send(mass_s.at[0], mass_r.at[0], m_send, m_recv, 0, twin)
 
     a1[0].wait_recv()
     a1[1].wait_recv()
@@ -205,15 +197,22 @@
                 send(b2_s.at[1], b2_r.at[1], rs_send, rs_recv, 11, left),
             ]
 
-    mass_twin.wait_recv()
-    mass_s[1] = mass_s[0] + mass_r[0]
-    mass_over = send(mass_s.at[1], mass_r.at[1], m_send, m_recv, 1, over)
-    kc[3].wait_recv()
-    kc.append(kkt_send(3, 1, half0, right, 7))
-    kc[4].wait_recv()
-    kc.append(kkt_send(1, 1, half1, left, 8))
     for copy in others:
         copy.wait()
+
+    mass_over.wait_recv()
+    mass_s[2] = mass_s[1] + mass_r[1]
+    mass_z = [
+        send(mass_s.at[2], mass_r.at[2], m_send, m_recv, 2, up),
+        send(mass_s.at[2], mass_r.at[3], m_send, m_recv, 3, down),
+    ]
+    demand_t = demand_v[...].T
+    a2[0, 1].wait_recv()
+    a2[1, 1].wait_recv()
+    a3_s[...] = (
+        part[1, 0, 0:RA] + a2_r[0, 1].astype(f32) + a2_r[1, 1].astype(f32)
+    ).astype(bf16)
+    a3 = send(a3_s, a3_r, rs_send, rs_recv, 14, across)
 
     b1[1].wait_recv()
     b2[0].wait_recv()
@@ -230,21 +229,7 @@
     ).astype(bf16)
     b3.append(send(b3_s.at[1], b3_r.at[1], rs_send, rs_recv, 13, left))
 
-    a2[0, 1].wait_recv()
-    a2[1, 1].wait_recv()
-    a3_s[...] = (
-        part[1, 0, 0:RA] + a2_r[0, 1].astype(f32) + a2_r[1, 1].astype(f32)
-    ).astype(bf16)
-    a3 = send(a3_s, a3_r, rs_send, rs_recv, 14, across)
-
-    mass_over.wait_recv()
-    mass_s[2] = mass_s[1] + mass_r[1]
-    mass_z = [
-        send(mass_s.at[2], mass_r.at[2], m_send, m_recv, 2, up),
-        send(mass_s.at[2], mass_r.at[3], m_send, m_recv, 3, down),
-    ]
-
-    for k in range(5, 9):
+    for k in range(1, 7):
         kc[k].wait_recv()
 
     @pl.loop(0, ROWS // CH)
@@ -266,15 +251,10 @@
     mass_z[0].wait_recv()
     mass_z[1].wait_recv()
     mass_z.append(send(mass_s.at[2], mass_r.at[4], m_send, m_recv, 4, peer(0, 2)))
-    lc = [
-        link_send(0, 0, over, 0),
-        link_send(0, 0, up, 1),
-        link_send(0, 0, down, 2),
-        link_send(0, 0, peer(0, 2), 3),
-    ]
+    lc = {k: link_send(0, 0, to, k) for k, to in ((1, up), (2, down), (3, peer(0, 2)))}
     tc = [twin_send(0, 0, 0)]
-
-    demand_t = demand_v[...].T
+    lc[0] = link_send(0, 0, over, 0)
+
     own = pl.ds(pl.multiple_of(d * B, B), B)
     b1[0].wait_recv()
     b3[0].wait_recv()
@@ -360,9 +340,9 @@
     ).astype(bf16)
     low_1()
     lc[0].wait_recv()
-    lc.append(link_send(1, 0, up, 4))
-    lc.append(link_send(1, 0, down, 5))
-    lc.append(link_send(1, 0, peer(0, 2), 6))
+    lc[4] = link_send(1, 0, up, 4)
+    lc[5] = link_send(1, 0, down, 5)
+    lc[6] = link_send(1, 0, peer(0, 2), 6)
     tc.append(twin_send(1, 0, 1))
     turn_1()
     rest_1()
@@ -425,11 +405,7 @@
 
     join(0)
     slice_copy(1, 0).start()
-    write_planned = pltpu.make_async_copy(planned_v, planned_out, out_sem.at[1])
-    write_planned.start()
     rec_own[...] = nt(kkt_v[...], rhs[...]).astype(bf16)
-    write_rec = pltpu.make_async_copy(rec_own, recourse_out, out_sem.at[0])
-    write_rec.start()
     mass_z[2].wait_recv()
     mass = mass_s[2] + mass_r[2] + mass_r[3] + mass_r[4]
     total = tot[0, pl.ds(pl.multiple_of(core * (CH // 2) + yh * SLICE, SLICE), SLICE), :]
@@ -454,9 +430,7 @@
         c.append(send(cons_b.at[theirs], cons_b.at[theirs], c_send, c_recv, k, twin))
     for copy in c:
         copy.wait_recv()
-    write_cons = pltpu.make_async_copy(cons_b, cons_out, out_sem.at[2])
-    write_cons.start()
-
+    cons_out[...] = cons_b[...]
     for copy in started:
         copy.wait_send()
     for oz in range(4):
@@ -464,45 +438,37 @@
         for oy in range(2):
             if oz or oy:
                 slice_copy(oy, oz).wait_send()
-    write_rec.wait()
-    write_planned.wait()
-    write_cons.wait()
 
 
 def last_kernel(
-    planned_hbm, recourse_hbm, cons_hbm, mult_hbm, node_ref,
+    planned_ref, recourse_ref, cons_ref, mult_ref, node_ref,
     planned_out, recourse_out, cons_out, next_out,
-    planned_v, recourse_v, cons_v, mult_v, cons_f, member, load, out_sem,
+    cons_f, next_v, member, out_sem,
 ):
-    pairs = ((planned_hbm, planned_v), (recourse_hbm, recourse_v), (cons_hbm, cons_v))
-    loads = [pltpu.make_async_copy(a, b, load.at[k]) for k, (a, b) in enumerate(pairs)]
-    loads.append(pltpu.make_async_copy(mult_hbm, mult_v, load.at[3]))
-    for copy in loads:
+    writes = [
+        pltpu.make_async_copy(planned_ref, planned_out, out_sem.at[0]),
+        pltpu.make_async_copy(recourse_ref, recourse_out, out_sem.at[1]),
+    ]
+    for copy in writes:
         copy.start()
     node_ids = lax.broadcasted_iota(jnp.int32, (G, S), 0)
     member[...] = jnp.where(node_ids == node_ref[...], 1.0, 0.0).astype(bf16)
-    loads[0].wait()
-    writes = [pltpu.make_async_copy(planned_v, planned_out, out_sem.at[0])]
-    writes[0].start()
-    loads[1].wait()
-    writes.append(pltpu.make_async_copy(recourse_v, recourse_out, out_sem.at[1]))
-    writes[1].start()
-    loads[2].wait()
-    loads[3].wait()
 
     def put(j):
         rows = pl.ds(pl.multiple_of(j * CH, CH), CH)
         return (
             pltpu.make_async_copy(cons_f.at[rows], cons_out.at[rows], out_sem.at[2 + j]),
-            pltpu.make_async_copy(mult_v.at[rows], next_out.at[rows], out_sem.at[6 + j]),
+            pltpu.make_async_copy(next_v.at[rows], next_out.at[rows], out_sem.at[6 + j]),
         )
 
     @pl.loop(0, ROWS // CH)
     def _(j):
         rows = pl.ds(pl.multiple_of(j * CH, CH), CH)
-        spread = nn(cons_v[rows, :], member[...])
-        cons_f[rows, :] = cons_v[rows, :].astype(f32)
-        mult_v[rows, :] = mult_v[rows, :] + PENALTY * (planned_v[rows, :].astype(f32) - spread)
+        spread = nn(cons_ref[rows, :], member[...])
+        cons_f[rows, :] = cons_ref[rows, :].astype(f32)
+        next_v[rows, :] = mult_ref[rows, :] + PENALTY * (
+            planned_ref[rows, :].astype(f32) - spread
+        )
         for copy in put(j):
             copy.start()
 
@@ -518,7 +484,6 @@
 ):
     any_space = pl.BlockSpec(memory_space=pl.ANY)
     vmem = pl.BlockSpec(memory_space=pltpu.VMEM)
-    hbm = pl.BlockSpec(memory_space=pltpu.HBM)
     V = pltpu.VMEM
     D = pltpu.SemaphoreType.DMA
     scratch = [
@@ -531,28 +496,24 @@
         V((4, RB, B), bf16), V((4, RB, B), bf16),
         V((2, HB, B), bf16), V((2, HB, B), bf16),
         V((2, RB, B), bf16), V((2, RB, B), bf16),
-        V((S, M), bf16), V((ROWS, M), bf16), V((M, PIECE), bf16), V((B, S), bf16),
+        V((S, M), bf16), V((ROWS, M), bf16), V((M, PIECE), bf16),
         V((G, S), bf16), V((3, 8, G), f32), V((5, 8, G), f32),
-        V((ROWS, S), bf16), V((4, CH, G), f32),
+        V((4, CH, G), f32),
         V((4, CH // 2, G), bf16), V((4, CH // 2, G), bf16),
         V((4, CH // 2, G), bf16), V((8, SLICE, G), bf16), V((ROWS, G), bf16),
-        D((6,)), D((8,)), D((3,)),
-        D((15,)), D((15,)), D((18,)), D((18,)), D((9,)), D((9,)), D((7,)), D((7,)), D((8,)), D((8,)),
+        D((6,)), D((8,)),
+        D((15,)), D((15,)), D((18,)), D((18,)), D((7,)), D((7,)), D((7,)), D((7,)), D((8,)), D((8,)),
         D((5,)), D((5,)), D((4,)), D((4,)), D((8,)), D((8,)), D((7,)), D((7,)), D((8,)), D((8,)),
     ]
     node_row = scenario_node.reshape(1, S)
     planned, recourse, consensus = pl.pallas_call(
         kernel,
-        out_shape=(
-            jax.ShapeDtypeStruct((ROWS, S), bf16),
-            jax.ShapeDtypeStruct((B, S), bf16),
-            jax.ShapeDtypeStruct((ROWS, G), bf16),
-        ),
+        out_shape=(V((ROWS, S), bf16), V((B, S), bf16), V((ROWS, G), bf16)),
         in_specs=[any_space] * 6 + [vmem] * 2,
-        out_specs=(any_space,) * 3,
+        out_specs=(vmem,) * 3,
         scratch_shapes=scratch,
         compiler_params=pltpu.CompilerParams(
-            collective_id=0, has_side_effects=True, vmem_limit_bytes=56 * 2**20
+            collective_id=0, has_side_effects=True, vmem_limit_bytes=57 * 2**20
         ),
     )(
         order_qty, multiplier, unit_cost, demand, technology, kkt_inverse,
@@ -567,13 +528,12 @@
                 jax.ShapeDtypeStruct((ROWS, G), f32),
                 jax.ShapeDtypeStruct((ROWS, S), f32),
             ),
-            in_specs=[hbm] * 4 + [vmem],
+            in_specs=[vmem] * 5,
             out_specs=(any_space,) * 4,
             scratch_shapes=[
-                V((ROWS, S), bf16), V((B, S), bf16), V((ROWS, G), bf16), V((ROWS, S), f32),
-                V((ROWS, G), f32), V((G, S), bf16), D((4,)), D((10,)),
+                V((ROWS, G), f32), V((ROWS, S), f32), V((G, S), bf16), D((10,)),
             ],
-            compiler_params=pltpu.CompilerParams(vmem_limit_bytes=60 * 2**20),
+            compiler_params=pltpu.CompilerParams(vmem_limit_bytes=24 * 2**20),
         )(planned, recourse, consensus, multiplier, node_row)
     )
 

time: 84 us -> 78.9 us (0.939)
  Pallas kernels: 83.2 us -> 78.1 us
    pallas_call x1, Pallas kernels: 5.51 us -> 2.51 us  [on_device(): pl.pallas_call(last_kernel, out_shape=(jax.ShapeDtypeStruct((ROWS, S), bf...]
    pallas_call x1, Pallas kernels: 77.6 us -> 75.6 us  [on_device(): pl.pallas_call(kernel, out_shape=(V((ROWS, S), bf16), V((B, S), bf16), V(...]
where the time goes in v4:
time: 78.9 us; the launch traced here: 78.8 us
  Pallas kernels  78.1 us (99%)
    pallas_call x1, Pallas kernels, on_device(): pl.pallas_call(kernel, out_shape=(V((ROWS, S), bf16), V((B, S), bf16), V(...  75.6 us
    pallas_call x1, Pallas kernels, on_device(): pl.pallas_call(last_kernel, out_shape=(jax.ShapeDtypeStruct((ROWS, S), bf...  2.51 us

profile of v4, /device:TPU:1, one launch (start us, length us, event | category | flops | bytes accessed | tf_op | source)
XLA Modules:
  0.0 78.8 jit_solution(17583677450925397860)
XLA Ops:
  0.6 0.0 copy-start
  0.6 0.0 copy-start.1
  0.7 75.6 %shard_map.111 = (bf16[1024,512]{1,0:T(8,128)(2,1)S(1)}, bf16[256,512]{1,0:T(8,128)(2,1)S(1)}, bf16[1024,512]{1,0:T(8,128)(2,1)S(1)}) custom-call(bf16[1024,512]{1,0:T(8,128)(2,1)} %order_hbm.1, f32[1024,512]{1,0:T(8,128)} %mult_ref.1, bf16[1024,512]{1,0:T(8,128)(2,1)} %cost_hbm.1, bf16[256,512]{1,0:T(8,128)(2,1)} %demand_hbm.1, ...), custom_call_target="tpu_custom_call" | custom-call | tf_op jit(solution)/shard_map/pallas_call | solution.py:509
  76.3 0.0 copy-done
  76.3 0.0 copy-done.1
  76.3 2.5 %shard_map.112 = (bf16[1024,512]{1,0:T(8,128)(2,1)}, bf16[256,512]{1,0:T(8,128)(2,1)}, f32[1024,512]{1,0:T(8,128)}, f32[1024,512]{1,0:T(8,128)}) custom-call(bf16[1024,512]{1,0:T(8,128)(2,1)S(1)} %get-tuple-element.7.planned_ref, bf16[256,512]{1,0:T(8,128)(2,1)S(1)} %get-tuple-element.8.recourse_ref, bf16[1024,512]{1,0:T(8,128)(2,1)S(1)} %get-tuple-element.9.cons_ref, ...), custom_call_target="tpu_custom_call" | custom-call | tf_op jit(solution)/shard_map/pallas_call | solution.py:523
Async XLA Ops:
  0.6 75.7 %copy-start = (f32[1024,512]{1,0:T(8,128)S(1)}, f32[1024,512]{1,0:T(8,128)}, u32[]{:S(2)}) copy-start(f32[1024,512]{1,0:T(8,128)} %mult_ref.1) | copy-start | bytes 6291460
  0.6 75.7 %copy-start.1 = (s32[512,1]{0,1:T(1,128)S(1)}, s32[512,1]{0,1:T(1,128)}, u32[]{:S(2)}) copy-start(s32[512,1]{0,1:T(1,128)} %param.15) | copy-start | bytes 6148

commit v5 on v4

--- a/solution.py
+++ b/solution.py
@@ -17,7 +17,7 @@
 CH = 256
 PIECE = M // 16
 
-RA = 288
+RA = 256
 HA = RA // 2
 RB = S - RA
 HB = RB // 2
@@ -42,7 +42,7 @@
     part,
     a1_s, a1_r, a2_s, a2_r, a3_s, a3_r,
     b1_s, b1_r, b2_s, b2_r, b3_s, b3_r,
-    rhs, link, kkt_cols,
+    rhs, link, kkt_cols, known,
     weight, mass_s, mass_r,
     tot, e1_s, e1_r, e2_s, e2_r, cons_b,
     load, tload,
@@ -339,6 +339,14 @@
         )
     ).astype(bf16)
     low_1()
+
+    @pl.loop(0, ROWS // CH)
+    def _(j):
+        rows = pl.ds(pl.multiple_of(j * CH, CH), CH)
+        known[rows, :] = order_v[rows, :].astype(f32) - STEP * (
+            cost_v[rows, :].astype(f32) + mult_v[rows, :]
+        )
+
     lc[0].wait_recv()
     lc[4] = link_send(1, 0, up, 4)
     lc[5] = link_send(1, 0, down, 5)
@@ -359,8 +367,7 @@
 
     def plan(rows):
         linked = nt(link[rows, :], rhs[...])
-        gradient = cost_v[rows, :].astype(f32) + mult_v[rows, :] + linked
-        planned = jnp.maximum(order_v[rows, :].astype(f32) - STEP * gradient, 0.0).astype(bf16)
+        planned = jnp.maximum(known[rows, :] - STEP * linked, 0.0).astype(bf16)
         planned_v[rows, :] = planned
         return nt(planned, weight[...])
 
@@ -496,7 +503,7 @@
         V((4, RB, B), bf16), V((4, RB, B), bf16),
         V((2, HB, B), bf16), V((2, HB, B), bf16),
         V((2, RB, B), bf16), V((2, RB, B), bf16),
-        V((S, M), bf16), V((ROWS, M), bf16), V((M, PIECE), bf16),
+        V((S, M), bf16), V((ROWS, M), bf16), V((M, PIECE), bf16), V((ROWS, S), f32),
         V((G, S), bf16), V((3, 8, G), f32), V((5, 8, G), f32),
         V((4, CH, G), f32),
         V((4, CH // 2, G), bf16), V((4, CH // 2, G), bf16),

time: 78.9 us -> 78.2 us (level)
  no operation moved by 1% of the time
where the time goes in v5:
time: 78.2 us; the launch traced here: 78 us
  Pallas kernels  77.4 us (99%)
    pallas_call x1, Pallas kernels, on_device(): pl.pallas_call(kernel, out_shape=(V((ROWS, S), bf16), V((B, S), bf16), V(...  74.9 us
    pallas_call x1, Pallas kernels, on_device(): pl.pallas_call(last_kernel, out_shape=(jax.ShapeDtypeStruct((ROWS, S), bf...  2.51 us

profile of v5, /device:TPU:1, one launch (start us, length us, event | category | flops | bytes accessed | tf_op | source)
XLA Modules:
  0.0 78.0 jit_solution(17130694539425471562)
XLA Ops:
  0.6 0.0 copy-start
  0.6 0.0 copy-start.1
  0.7 74.9 %shard_map.111 = (bf16[1024,512]{1,0:T(8,128)(2,1)S(1)}, bf16[256,512]{1,0:T(8,128)(2,1)S(1)}, bf16[1024,512]{1,0:T(8,128)(2,1)S(1)}) custom-call(bf16[1024,512]{1,0:T(8,128)(2,1)} %order_hbm.1, f32[1024,512]{1,0:T(8,128)} %mult_ref.1, bf16[1024,512]{1,0:T(8,128)(2,1)} %cost_hbm.1, bf16[256,512]{1,0:T(8,128)(2,1)} %demand_hbm.1, ...), custom_call_target="tpu_custom_call" | custom-call | tf_op jit(solution)/shard_map/pallas_call | solution.py:516
  75.5 0.0 copy-done
  75.5 0.0 copy-done.1
  75.5 2.5 %shard_map.112 = (bf16[1024,512]{1,0:T(8,128)(2,1)}, bf16[256,512]{1,0:T(8,128)(2,1)}, f32[1024,512]{1,0:T(8,128)}, f32[1024,512]{1,0:T(8,128)}) custom-call(bf16[1024,512]{1,0:T(8,128)(2,1)S(1)} %get-tuple-element.7.planned_ref, bf16[256,512]{1,0:T(8,128)(2,1)S(1)} %get-tuple-element.8.recourse_ref, bf16[1024,512]{1,0:T(8,128)(2,1)S(1)} %get-tuple-element.9.cons_ref, ...), custom_call_target="tpu_custom_call" | custom-call | tf_op jit(solution)/shard_map/pallas_call | solution.py:530
Async XLA Ops:
  0.6 74.9 %copy-start = (f32[1024,512]{1,0:T(8,128)S(1)}, f32[1024,512]{1,0:T(8,128)}, u32[]{:S(2)}) copy-start(f32[1024,512]{1,0:T(8,128)} %mult_ref.1) | copy-start | bytes 6291460
  0.6 74.9 %copy-start.1 = (s32[512,1]{0,1:T(1,128)S(1)}, s32[512,1]{0,1:T(1,128)}, u32[]{:S(2)}) copy-start(s32[512,1]{0,1:T(1,128)} %param.15) | copy-start | bytes 6148
